TPU v7x, 128 devices: a whole 4x4x4 slice. The times are simulated.
128 devices in a mesh: gx: 8 (over z, core), gy: 16 (over y, x).
Axes of the slice: x: 4, y: 4, z: 4, core: 2. Of those that a mesh axis runs over, the one named last changes fastest.
Arguments:
- e_adjoint: float32 [3, 256, 640, 128], P(None, 'gx', 'gy'), may hold values from -6 to 6
- h_adjoint: float32 [3, 256, 640, 128], P(None, 'gx', 'gy'), may hold values from -6 to 6
- conductivity: float32 [256, 640, 128], P('gx', 'gy'), may hold values from 0.05 to 2
- permittivity: float32 [256, 640, 128], P('gx', 'gy'), may hold values from 1 to 4
- forward_e: bfloat16 [3, 3, 256, 640, 128], P(None, None, 'gx', 'gy'), may hold values from -6 to 6
- receiver_data: float32 [131072, 128], P(('gx', 'gy')), may hold values from -6 to 6
- receiver_tile: int32 [131072, 1], P(('gx', 'gy')), may hold values from 0 to 127; in each aligned block of 1024 rows (0 to 1023, 1024 to 2047, ...) at most 24 rows name the same one
- receiver_cell: int32 [131072], P(('gx', 'gy')), may hold values from 0 to 163839
- receiver_comp: int32 [131072], P(('gx', 'gy')), may hold values from 0 to 2
Outputs:
- e_final: float32 [3, 256, 640, 128], P(None, 'gx', 'gy')
- h_final: float32 [3, 256, 640, 128], P(None, 'gx', 'gy')
- grad_sigma: float32 [256, 640, 128], P('gx', 'gy')
Inputs may be any that keep to these rules, and one draw needn't show every extreme that they name: `receiver_tile`: among the rows of one device, no tile is named by more than 24 rows.
All inputs are finite; a program needn't handle non-finite values.
Results may differ from a plain program's by a relative error of at most 0.0003.
Values sent between devices are 32-bit elements; how exact they have to be, the bound alone decides.
A program may use at most 128 MiB of HBM per device.

v0:
```python
import functools

import jax
import jax.numpy as jnp
from jax import lax
from jax.experimental import pallas as pl
from jax.experimental.pallas import tpu as pltpu
from jax.sharding import PartitionSpec as P

STEPS = 3
SAMPLES = 128
LANES = 128
FIELDS = 4
SPAN = LANES // FIELDS
MESH = pl.DeviceIdType.MESH
MIB = 1 << 20

time_step = 0.55


def split3(x):
    a = x.astype(jnp.bfloat16)
    rest = x - a.astype(jnp.float32)
    b = rest.astype(jnp.bfloat16)
    c = (rest - b.astype(jnp.float32)).astype(jnp.bfloat16)
    return a, b, c


def mm(a, b, contract=((1,), (0,))):
    return lax.dot_general(a, b, (contract, ((), ())), preferred_element_type=jnp.float32)


def time_kernel():
    rows = 8
    sample = lax.broadcasted_iota(jnp.int32, (rows, SAMPLES), 1).astype(jnp.float32)
    step = lax.broadcasted_iota(jnp.int32, (rows, SAMPLES), 0).astype(jnp.float32)
    centre = (step + 0.5) * (SAMPLES / STEPS)
    spread = SAMPLES / (4.0 * STEPS)
    kernel = jnp.exp(-jnp.square((sample - centre) / spread))
    kernel = jnp.where(step < STEPS - 0.5, kernel, 0.0)
    norm = jnp.sum(kernel * kernel, axis=1, keepdims=True)
    return kernel / jnp.sqrt(jnp.where(norm > 0.0, norm, 1.0))


def pack(devices, cells, data_ref, tile_ref, cell_ref, comp_ref):
    blocks, width = tile_ref.shape
    kernel = time_kernel()
    before = (
        lax.broadcasted_iota(jnp.int32, (width, width), 0)
        < lax.broadcasted_iota(jnp.int32, (width, width), 1)
    ).astype(jnp.bfloat16)
    every = jnp.ones((width, width), jnp.bfloat16)
    destination = lax.broadcasted_iota(jnp.int32, (devices, width), 0)
    slot = lax.broadcasted_iota(jnp.int32, (SPAN, width), 0).astype(jnp.float32)
    seen = jnp.zeros((devices, width), jnp.float32)
    packed = jnp.zeros((devices, LANES), jnp.float32)
    for b in range(blocks):
        onehot = (destination == tile_ref[b : b + 1, :]).astype(jnp.float32)
        hot = onehot.astype(jnp.bfloat16)
        rank = jnp.sum(onehot * (seen + mm(hot, before)), axis=0, keepdims=True)
        seen = seen + mm(hot, every)
        amplitude = lax.dot_general(
            kernel,
            data_ref[b * width : (b + 1) * width, :],
            (((1,), (1,)), ((), ())),
            precision=lax.Precision.HIGHEST,
            preferred_element_type=jnp.float32,
        )
        code = (comp_ref[b : b + 1, :] * cells + cell_ref[b : b + 1, :]).astype(jnp.float32)
        here = slot == rank
        fields = [amplitude[t : t + 1, :] for t in range(STEPS)] + [code]
        spread = jnp.concatenate([jnp.where(here, f, 0.0) for f in fields], axis=0)
        for term in split3(spread):
            packed = packed + mm(hot, term, ((1,), (1,)))
    return packed


def route_kernel(
    nx,
    ny,
    cells,
    data_ref,
    tile_ref,
    cell_ref,
    comp_ref,
    got_ref,
    code_ref,
    first,
    mid,
    second,
    last,
    send_y,
    recv_y,
    send_x,
    recv_x,
):
    ix, iy = lax.axis_index("gx"), lax.axis_index("gy")
    barrier = pltpu.get_barrier_semaphore()
    for k in range(1, nx):
        pl.semaphore_signal(barrier, inc=1, device_id=(lax.rem(ix + k, nx), iy), device_id_type=MESH)
    for k in range(1, ny):
        pl.semaphore_signal(barrier, inc=1, device_id=(ix, lax.rem(iy + k, ny)), device_id_type=MESH)

    first[...] = pack(nx * ny, cells, data_ref, tile_ref, cell_ref, comp_ref)
    pl.semaphore_wait(barrier, nx + ny - 2)

    copies = []
    for k in range(1, nx):
        to = lax.rem(ix + k, nx)
        copy = pltpu.make_async_remote_copy(
            src_ref=first.at[pl.ds(pl.multiple_of(to * ny, ny), ny), :],
            dst_ref=mid.at[pl.ds(pl.multiple_of(ix * ny, ny), ny), :],
            send_sem=send_x.at[k - 1],
            recv_sem=recv_x.at[k - 1],
            device_id=(to, iy),
            device_id_type=MESH,
        )
        copy.start()
        copies.append(copy)
    own = pl.ds(pl.multiple_of(ix * ny, ny), ny)
    mid[own, :] = first[own, :]
    for copy in copies:
        copy.wait_recv()
    for j in range(ny):
        second[j * nx : (j + 1) * nx, :] = mid[pl.ds(j, nx, stride=ny), :]
    later = []
    for k in range(1, ny):
        to = lax.rem(iy + k, ny)
        copy = pltpu.make_async_remote_copy(
            src_ref=second.at[pl.ds(pl.multiple_of(to * nx, nx), nx), :],
            dst_ref=last.at[pl.ds(pl.multiple_of(iy * nx, nx), nx), :],
            send_sem=send_y.at[k - 1],
            recv_sem=recv_y.at[k - 1],
            device_id=(ix, to),
            device_id_type=MESH,
        )
        copy.start()
        later.append(copy)
    own = pl.ds(pl.multiple_of(iy * nx, nx), nx)
    last[own, :] = second[own, :]
    for copy in copies:
        copy.wait_send()
    for copy in later:
        copy.wait()
    got = last[...]
    got_ref[...] = got
    code_ref[...] = got.astype(jnp.int32)


def route(nx, ny, cells, data, tile, cell, comp):
    devices = nx * ny
    rows = lambda: pltpu.VMEM((devices, LANES), jnp.float32)
    return pl.pallas_call(
        functools.partial(route_kernel, nx, ny, cells),
        out_shape=[
            jax.ShapeDtypeStruct((devices, LANES), jnp.float32),
            jax.ShapeDtypeStruct((devices, LANES), jnp.int32),
        ],
        in_specs=[pl.BlockSpec(memory_space=pltpu.VMEM)] * 4,
        out_specs=[pl.BlockSpec(memory_space=pltpu.VMEM)] * 2,
        scratch_shapes=[
            rows(),
            rows(),
            rows(),
            rows(),
            pltpu.SemaphoreType.DMA((ny - 1,)),
            pltpu.SemaphoreType.DMA((ny - 1,)),
            pltpu.SemaphoreType.DMA((nx - 1,)),
            pltpu.SemaphoreType.DMA((nx - 1,)),
        ],
        compiler_params=pltpu.CompilerParams(
            collective_id=0, has_side_effects=True, vmem_limit_bytes=16 * MIB
        ),
        name="route",
    )(data, tile, cell, comp)


def scatter_kernel(cap, code_ref, got_ref, out_ref, quad, wide):
    devices = got_ref.shape[0]
    got = got_ref[...]
    lane = lax.broadcasted_iota(jnp.int32, (devices, LANES), 1)
    slot = jnp.bitwise_and(lane, SPAN - 1)
    codes = jnp.where(lane >= (FIELDS - 1) * SPAN, got, 0.0)
    codes = codes + pltpu.roll(codes, SPAN, 1)
    codes = codes + pltpu.roll(codes, 2 * SPAN, 1)
    total = got
    for d in range(1, cap):
        same = (codes == pltpu.roll(codes, d, 1)) & (slot >= d)
        total = total + jnp.where(same, pltpu.roll(got, d, 1), 0.0)
    for t in range(FIELDS):
        quad[pl.ds(t, devices, stride=FIELDS), :] = jnp.where(
            (lane >= t * SPAN) & (lane < (t + 1) * SPAN), total, 0.0
        )
    values = quad[...]
    high = values.astype(jnp.bfloat16)
    low = (values - high.astype(jnp.float32)).astype(jnp.bfloat16)
    terms = jnp.concatenate([high, low], axis=1)
    row_slot = jnp.bitwise_and(lax.broadcasted_iota(jnp.int32, (2 * LANES, 2 * LANES), 0), SPAN - 1)
    column = lax.broadcasted_iota(jnp.int32, (2 * LANES, 2 * LANES), 1) // LANES
    for i in range(0, cap, 2):
        pick = (row_slot == column + i).astype(jnp.bfloat16)
        both = mm(terms, pick)
        wide[i] = both[:, :LANES]
        wide[i + 1] = both[:, LANES:]

    rows = out_ref.shape[0]
    step = 128

    def clear(n, _):
        out_ref[pl.ds(pl.multiple_of(n * step, step), step), :] = jnp.zeros((step, LANES), jnp.float32)
        return 0

    lax.fori_loop(0, rows // step, clear, 0)
    depth = lax.broadcasted_iota(jnp.int32, (FIELDS, LANES), 1)

    def place(s, _):
        where, news = [], []
        for i in range(cap):
            code = code_ref[s, (FIELDS - 1) * SPAN + i]
            row = pl.ds(pl.multiple_of(lax.shift_right_logical(code, 7) * FIELDS, FIELDS), FIELDS)
            news.append(out_ref[row, :] + wide[i, pl.ds(pl.multiple_of(s * FIELDS, FIELDS), FIELDS), :])
            where.append((row, depth == jnp.bitwise_and(code, LANES - 1)))
        for (row, mask), new in zip(where, news):
            pltpu.store(out_ref.at[row, :], new, mask=mask)
        return 0

    lax.fori_loop(0, devices, place, 0)


def scatter(cap, rows, codes, got):
    devices = got.shape[0]
    return pl.pallas_call(
        functools.partial(scatter_kernel, cap),
        out_shape=jax.ShapeDtypeStruct((rows * FIELDS, LANES), jnp.float32),
        in_specs=[pl.BlockSpec(memory_space=pltpu.SMEM), pl.BlockSpec(memory_space=pltpu.VMEM)],
        out_specs=pl.BlockSpec(memory_space=pltpu.VMEM),
        scratch_shapes=[
            pltpu.VMEM((devices * FIELDS, LANES), jnp.float32),
            pltpu.VMEM((cap, devices * FIELDS, LANES), jnp.float32),
        ],
        compiler_params=pltpu.CompilerParams(vmem_limit_bytes=32 * MIB),
        name="scatter",
    )(codes, got)


def steps_kernel(
    nx,
    ny,
    e_in,
    h_in,
    cond_in,
    perm_in,
    fwd_in,
    src_in,
    e,
    h,
    grad,
    decay,
    gain,
    fwd,
    src,
    ex_got,
    ey_got,
    hx_got,
    hy_got,
    ex_put,
    ey_put,
    hx_put,
    hy_put,
    load,
    send,
    recv,
):
    ix, iy = lax.axis_index("gx"), lax.axis_index("gy")
    below_x = (lax.rem(ix + nx - 1, nx), iy)
    above_x = (lax.rem(ix + 1, nx), iy)
    below_y = (ix, lax.rem(iy + ny - 1, ny))
    above_y = (ix, lax.rem(iy + 1, ny))
    barrier = pltpu.get_barrier_semaphore()
    for other in (below_x, above_x, below_y, above_y):
        pl.semaphore_signal(barrier, inc=1, device_id=other, device_id_type=MESH)

    loads = [
        pltpu.make_async_copy(a, b, load.at[n])
        for n, (a, b) in enumerate(
            (
                (e_in, e),
                (h_in, h),
                (cond_in, decay),
                (perm_in, gain),
                (src_in, src),
                (fwd_in, fwd),
            )
        )
    ]
    for copy in loads:
        copy.start()

    size_x, size_y, depth = e.shape[1:]
    shape = (size_y, depth)
    row = lax.broadcasted_iota(jnp.int32, shape, 0)
    lane = lax.broadcasted_iota(jnp.int32, shape, 1)
    one = jnp.float32(1.0)
    zero = jnp.float32(0.0)
    keep_ex = jnp.where(ix == nx - 1, zero, one)
    keep_ey = jnp.where(iy == ny - 1, zero, one)
    keep_hx = jnp.where(ix == 0, zero, one)
    keep_hy = jnp.where(iy == 0, zero, one)

    def up_z(f):
        return jnp.where(lane == depth - 1, 0.0, pltpu.roll(f, depth - 1, 1))

    def down_z(f):
        return jnp.where(lane == 0, 0.0, pltpu.roll(f, 1, 1))

    def up_y(f, after):
        return jnp.where(row == size_y - 1, after, pltpu.roll(f, size_y - 1, 0))

    def down_y(f, before):
        return jnp.where(row == 0, before, pltpu.roll(f, 1, 0))

    def e_rows(x, p, t, ex, ez):
        ey_put[t, 0, pl.ds(p, 1), :] = ex[:1]
        ey_put[t, 1, pl.ds(p, 1), :] = ez[:1]

    def h_plane(x, p, t, next_y, next_z):
        ex, ey, ez = e[0, x], e[1, x], e[2, x]
        after_x = ey_got[t, 0, pl.ds(p, 1), :] * keep_ey
        after_z = ey_got[t, 1, pl.ds(p, 1), :] * keep_ey
        curl_x = (up_y(ez, after_z) - ez) - (up_z(ey) - ey)
        curl_y = (up_z(ex) - ex) - (next_z - ez)
        curl_z = (next_y - ey) - (up_y(ex, after_x) - ex)
        hx = h[0, x] - time_step * curl_x
        hy = h[1, x] - time_step * curl_y
        hz = h[2, x] - time_step * curl_z
        h[0, x] = hx
        h[1, x] = hy
        h[2, x] = hz
        hy_put[t, 0, pl.ds(p, 1), :] = hx[size_y - 1 :]
        hy_put[t, 1, pl.ds(p, 1), :] = hz[size_y - 1 :]

    def e_plane(x, p, t, last_y, last_z):
        hx, hy, hz = h[0, x], h[1, x], h[2, x]
        before_x = hy_got[t, 0, pl.ds(p, 1), :] * keep_hy
        before_z = hy_got[t, 1, pl.ds(p, 1), :] * keep_hy
        curl_x = (hz - down_y(hz, before_z)) - (hy - down_z(hy))
        curl_y = (hx - down_z(hx)) - (hz - last_z)
        curl_z = (hy - last_y) - (hx - down_y(hx, before_x))
        if t == 0:
            half_loss = decay[x] * (0.5 * time_step)
            eps = gain[x]
            inverse = 1.0 / (eps + half_loss)
            fade = (eps - half_loss) * inverse
            rise = time_step * inverse
            decay[x] = fade
            gain[x] = rise
        else:
            fade, rise = decay[x], gain[x]
        total = None
        for c, curl in enumerate((curl_x, curl_y, curl_z)):
            source = src[c, x, pl.ds(t, size_y, stride=FIELDS), :]
            new = fade * e[c, x] + rise * (curl - source)
            e[c, x] = new
            term = fwd[t, c, x].astype(jnp.float32) * new
            total = term if total is None else total + term
            if t < STEPS - 1 and c != 1:
                ey_put[t + 1, c // 2, pl.ds(p, 1), :] = new[:1]
        grad[x] = total if t == 0 else grad[x] + total

    def remote(a, b, n, device):
        return pltpu.make_async_remote_copy(
            src_ref=a,
            dst_ref=b,
            send_sem=send.at[n],
            recv_sem=recv.at[n],
            device_id=device,
            device_id_type=MESH,
        )

    def e_copies(t):
        return (
            remote(ey_put.at[t], ey_got.at[t], 4 * t, below_y),
            remote(ex_put.at[t], ex_got.at[t], 4 * t + 1, below_x),
        )

    def h_copies(t):
        return (
            remote(hy_put.at[t], hy_got.at[t], 4 * t + 2, above_y),
            remote(hx_put.at[t], hx_got.at[t], 4 * t + 3, above_x),
        )

    loads[0].wait()

    def first_rows(p, _):
        x = lax.rem(p + 1, size_x)
        e_rows(x, p, 0, e[0, x], e[2, x])
        return 0

    lax.fori_loop(0, size_x, first_rows, 0)
    pl.semaphore_wait(barrier, 4)
    pending = []
    for t in range(STEPS):
        ex_put[t, 0] = e[1, 0]
        ex_put[t, 1] = e[2, 0]
        across, along = e_copies(t)
        across.start()
        along.start()
        if t == 0:
            loads[1].wait()
        across.wait_recv()

        def h_inner(p, _):
            x = p + 1
            h_plane(x, p, t, e[1, x + 1], e[2, x + 1])
            return 0

        lax.fori_loop(0, size_x - 2, h_inner, 0)
        along.wait_recv()
        h_plane(size_x - 1, size_x - 2, t, ex_got[t, 0] * keep_ex, ex_got[t, 1] * keep_ex)
        h_plane(0, size_x - 1, t, e[1, 1], e[2, 1])
        pending += [across, along]
        hx_put[t, 0] = h[1, size_x - 1]
        hx_put[t, 1] = h[2, size_x - 1]
        across, along = h_copies(t)
        across.start()
        along.start()
        if t == 0:
            for n in (2, 3, 4, 5):
                loads[n].wait()
        across.wait_recv()

        def e_inner(p, _):
            x = p + 1
            e_plane(x, p, t, h[1, x - 1], h[2, x - 1])
            return 0

        lax.fori_loop(0, size_x - 1, e_inner, 0)
        along.wait_recv()
        e_plane(0, size_x - 1, t, hx_got[t, 0] * keep_hx, hx_got[t, 1] * keep_hx)
        pending += [across, along]
    for copy in pending:
        copy.wait_send()


def steps(nx, ny, e, h, cond, perm, fwd, src):
    size_x, size_y, depth = e.shape[1:]
    field = jax.ShapeDtypeStruct(e.shape, jnp.float32)
    single = jax.ShapeDtypeStruct(cond.shape, jnp.float32)
    x_halo = lambda: pltpu.VMEM((STEPS, 2, size_y, depth), jnp.float32)
    y_halo = lambda: pltpu.VMEM((STEPS, 2, size_x, depth), jnp.float32)
    whole = lambda a: pltpu.VMEM(a.shape, a.dtype)
    return pl.pallas_call(
        functools.partial(steps_kernel, nx, ny),
        out_shape=[field, field, single],
        in_specs=[pl.BlockSpec(memory_space=pl.ANY)] * 6,
        out_specs=[pl.BlockSpec(memory_space=pltpu.VMEM)] * 3,
        scratch_shapes=[
            whole(cond),
            whole(perm),
            whole(fwd),
            whole(src),
            x_halo(),
            y_halo(),
            x_halo(),
            y_halo(),
            x_halo(),
            y_halo(),
            x_halo(),
            y_halo(),
            pltpu.SemaphoreType.DMA((6,)),
            pltpu.SemaphoreType.DMA((4 * STEPS,)),
            pltpu.SemaphoreType.DMA((4 * STEPS,)),
        ],
        compiler_params=pltpu.CompilerParams(
            collective_id=1, has_side_effects=True, vmem_limit_bytes=40 * MIB
        ),
        name="steps",
    )(e, h, cond, perm, fwd, src)


def per_device(
    e_adjoint,
    h_adjoint,
    conductivity,
    permittivity,
    forward_e,
    receiver_data,
    receiver_tile,
    receiver_cell,
    receiver_comp,
):
    _, size_x, size_y, depth = e_adjoint.shape
    nx, ny = lax.axis_size("gx"), lax.axis_size("gy")
    receivers = receiver_data.shape[0]
    cap = 3 * receivers // (nx * ny)
    by_lane = lambda a: a.reshape(receivers // LANES, LANES)
    got, codes = route(
        nx,
        ny,
        size_x * size_y * depth,
        receiver_data,
        by_lane(receiver_tile),
        by_lane(receiver_cell),
        by_lane(receiver_comp),
    )
    placed = scatter(cap, 3 * size_x * size_y, codes, got)
    placed = placed.reshape(3, size_x, size_y * FIELDS, depth)
    return tuple(steps(nx, ny, e_adjoint, h_adjoint, conductivity, permittivity, forward_e, placed))


def solution(mesh):
    placed = (
        P(None, "gx", "gy", None),
        P(None, "gx", "gy", None),
        P("gx", "gy", None),
        P("gx", "gy", None),
        P(None, None, "gx", "gy", None),
        P(("gx", "gy"), None),
        P(("gx", "gy"), None),
        P(("gx", "gy")),
        P(("gx", "gy")),
    )
    return jax.shard_map(
        per_device,
        mesh=mesh,
        in_specs=placed,
        out_specs=(P(None, "gx", "gy", None), P(None, "gx", "gy", None), P("gx", "gy", None)),
        check_vma=False,
    )
```

profile of v0, /device:TPU:0, one launch (start us, length us, event | category | flops | bytes accessed | tf_op | source)
XLA Modules:
  0.0 87.1 jit_solution(14504439079294336064)
XLA Ops:
  0.6 0.0 copy-start.6
  0.6 1.0 %copy-done.6 = f32[1024,128]{1,0:T(8,128)S(1)} copy-done((f32[1024,128]{1,0:T(8,128)S(1)}, f32[1024,128]{1,0:T(8,128)}, u32[]{:S(2)}) %copy-start.6) | copy-done | bytes 524312
  1.7 0.0 copy-start.7
  1.7 0.7 copy-done.7
  2.4 0.0 copy-start.8
  2.4 0.7 copy-done.8
  3.0 0.0 copy-start.9
  3.1 0.7 copy-done.9
  3.7 0.0 copy-start.5
  3.7 16.1 %route.1 = (f32[128,128]{1,0:T(8,128)S(1)}, s32[128,128]{1,0:T(8,128)S(1)}) custom-call(f32[1024,128]{1,0:T(8,128)S(1)} %copy-done.6, s32[8,128]{1,0:T(8,128)S(1)} %bitcast.5, s32[8,128]{1,0:T(8,128)S(1)} %bitcast.6, s32[8,128]{1,0:T(8,128)S(1)} %bitcast.7), custom_call_target="tpu_custom_call" | custom-call | tf_op jit(solution)/shard_map/route/pallas_call | solution.py:153
  19.9 0.0 copy-start.1
  19.9 0.0 copy-start.2
  19.9 0.0 copy-start.3
  19.9 0.0 copy-start.4
  19.9 13.3 %scatter.1 = f32[15360,128]{1,0:T(8,128)S(1)} custom-call(s32[128,128]{1,0:T(8,128)S(1)} %get-tuple-element.5.code_ref, f32[128,128]{1,0:T(8,128)S(1)} %get-tuple-element.6.got_ref), custom_call_target="tpu_custom_call" | custom-call | tf_op jit(solution)/shard_map/scatter/pallas_call | solution.py:232
  33.3 0.0 copy-start
  33.3 3.0 %copy-done = f32[15360,128]{1,0:T(8,128)} copy-done((f32[15360,128]{1,0:T(8,128)}, f32[15360,128]{1,0:T(8,128)S(1)}, u32[]{:S(2)}) %copy-start) | copy-done | bytes 7864344
  36.3 0.0 copy-done.5
  36.3 0.0 copy-done.1
  36.3 0.0 copy-done.2
  36.3 0.0 copy-done.3
  36.3 0.0 copy-done.4
  36.3 47.4 %steps.1 = (f32[3,32,40,128]{3,2,1,0:T(8,128)S(1)}, f32[3,32,40,128]{3,2,1,0:T(8,128)S(1)}, f32[32,40,128]{2,1,0:T(8,128)S(1)}) custom-call(f32[3,32,40,128]{3,2,1,0:T(8,128)S(1)} %copy-done.2, f32[3,32,40,128]{3,2,1,0:T(8,128)S(1)} %copy-done.3, f32[32,40,128]{2,1,0:T(8,128)S(1)} %copy-done.4, f32[32,40,128]{2,1,0:T(8,128)S(1)} %copy-done.5, ...), custom_call_target="tpu_custom_call" | custom-call | tf_op jit(solution)/shard_map/steps/pallas_call | solution.py:452
  83.7 1.3 %copy.15 = f32[3,32,40,128]{3,2,1,0:T(8,128)} copy(f32[3,32,40,128]{3,2,1,0:T(8,128)S(1)} %get-tuple-element.10) | data formatting | bytes 3932160
  85.0 1.3 %copy.16 = f32[3,32,40,128]{3,2,1,0:T(8,128)} copy(f32[3,32,40,128]{3,2,1,0:T(8,128)S(1)} %get-tuple-element.11) | data formatting | bytes 3932160
  86.3 0.8 copy.17
Async XLA Ops:
  0.6 1.0 %copy-start.6 = (f32[1024,128]{1,0:T(8,128)S(1)}, f32[1024,128]{1,0:T(8,128)}, u32[]{:S(2)}) copy-start(f32[1024,128]{1,0:T(8,128)} %data_ref.1) | copy-start | bytes 1572868
  1.7 0.7 copy-start.7
  2.4 0.7 copy-start.8
  3.0 0.7 copy-start.9
  3.7 32.6 %copy-start.5 = (f32[32,40,128]{2,1,0:T(8,128)S(1)}, f32[32,40,128]{2,1,0:T(8,128)}, u32[]{:S(2)}) copy-start(f32[32,40,128]{2,1,0:T(8,128)} %perm_in.1) | copy-start | bytes 1966084
  19.9 16.5 %copy-start.1 = (bf16[3,3,32,40,128]{4,3,2,1,0:T(8,128)(2,1)S(1)}, bf16[3,3,32,40,128]{4,3,2,1,0:T(8,128)(2,1)}, u32[]{:S(2)}) copy-start(bf16[3,3,32,40,128]{4,3,2,1,0:T(8,128)(2,1)} %fwd_in.1) | copy-start | bytes 8847364
  19.9 16.4 %copy-start.2 = (f32[3,32,40,128]{3,2,1,0:T(8,128)S(1)}, f32[3,32,40,128]{3,2,1,0:T(8,128)}, u32[]{:S(2)}) copy-start(f32[3,32,40,128]{3,2,1,0:T(8,128)} %e_in.1) | copy-start | bytes 5898244
  19.9 16.4 %copy-start.3 = (f32[3,32,40,128]{3,2,1,0:T(8,128)S(1)}, f32[3,32,40,128]{3,2,1,0:T(8,128)}, u32[]{:S(2)}) copy-start(f32[3,32,40,128]{3,2,1,0:T(8,128)} %h_in.1) | copy-start | bytes 5898244
  19.9 16.4 %copy-start.4 = (f32[32,40,128]{2,1,0:T(8,128)S(1)}, f32[32,40,128]{2,1,0:T(8,128)}, u32[]{:S(2)}) copy-start(f32[32,40,128]{2,1,0:T(8,128)} %cond_in.1) | copy-start | bytes 1966084
  33.3 3.1 %copy-start = (f32[15360,128]{1,0:T(8,128)}, f32[15360,128]{1,0:T(8,128)S(1)}, u32[]{:S(2)}) copy-start(f32[15360,128]{1,0:T(8,128)S(1)} %scatter.1) | copy-start | bytes 23592964
where the time goes:
time: 87.4 us; the launch traced here: 87.1 us
  Pallas kernels  76.9 us (88%)
  local copies, waits for them, and re-layouts  9.56 us (11%)
    pallas_call x1, Pallas kernels, steps(): pl.pallas_call(functools.partial(steps_kernel, nx, ny), out_shape=[field,...  47.4 us
    pallas_call x1, Pallas kernels, route(): pl.pallas_call(functools.partial(route_kernel, nx, ny, cells), out_shape=...  16.1 us
    pallas_call x1, Pallas kernels, scatter(): pl.pallas_call(functools.partial(scatter_kernel, cap), out_shape=jax.Shap...  13.3 us
    unnamed x23, local copies, waits for them, and re-layouts  9.56 us

commit v1 on v0

--- a/solution.py
+++ b/solution.py
@@ -13,6 +13,7 @@
 FIELDS = 4
 SPAN = LANES // FIELDS
 MESH = pl.DeviceIdType.MESH
+GROUP = 12
 MIB = 1 << 20
 
 time_step = 0.55
@@ -79,28 +80,39 @@
     nx,
     ny,
     cells,
+    data_in,
+    tile_in,
+    cell_in,
+    comp_in,
+    got_ref,
+    code_ref,
     data_ref,
     tile_ref,
     cell_ref,
     comp_ref,
-    got_ref,
-    code_ref,
     first,
     mid,
     second,
     last,
+    load,
     send_y,
     recv_y,
     send_x,
     recv_x,
 ):
     ix, iy = lax.axis_index("gx"), lax.axis_index("gy")
+    pairs = ((tile_in, tile_ref), (cell_in, cell_ref), (comp_in, comp_ref), (data_in, data_ref))
+    loads = [pltpu.make_async_copy(a, b, load.at[n]) for n, (a, b) in enumerate(pairs)]
+    for copy in loads:
+        copy.start()
     barrier = pltpu.get_barrier_semaphore()
     for k in range(1, nx):
         pl.semaphore_signal(barrier, inc=1, device_id=(lax.rem(ix + k, nx), iy), device_id_type=MESH)
     for k in range(1, ny):
         pl.semaphore_signal(barrier, inc=1, device_id=(ix, lax.rem(iy + k, ny)), device_id_type=MESH)
 
+    for copy in loads:
+        copy.wait()
     first[...] = pack(nx * ny, cells, data_ref, tile_ref, cell_ref, comp_ref)
     pl.semaphore_wait(barrier, nx + ny - 2)
 
@@ -142,9 +154,15 @@
         copy.wait_send()
     for copy in later:
         copy.wait()
-    got = last[...]
-    got_ref[...] = got
-    code_ref[...] = got.astype(jnp.int32)
+    got_ref[...] = last[...]
+    quarter = nx * ny // FIELDS
+    lane = lax.broadcasted_iota(jnp.int32, (quarter, LANES), 1) // SPAN
+    codes = jnp.zeros((quarter, LANES), jnp.int32)
+    for p in range(FIELDS):
+        code = last[pl.ds(p, quarter, stride=FIELDS), :].astype(jnp.int32)
+        word = jnp.bitwise_and(code, LANES - 1) + jnp.bitwise_and(code, -LANES) * FIELDS
+        codes = jnp.where(lane == p, pltpu.roll(word, (p + 1) * SPAN % LANES, 1), codes)
+    code_ref[...] = codes
 
 
 def route(nx, ny, cells, data, tile, cell, comp):
@@ -154,15 +172,17 @@
         functools.partial(route_kernel, nx, ny, cells),
         out_shape=[
             jax.ShapeDtypeStruct((devices, LANES), jnp.float32),
-            jax.ShapeDtypeStruct((devices, LANES), jnp.int32),
+            jax.ShapeDtypeStruct((devices // FIELDS, LANES), jnp.int32),
         ],
-        in_specs=[pl.BlockSpec(memory_space=pltpu.VMEM)] * 4,
+        in_specs=[pl.BlockSpec(memory_space=pltpu.HBM)] * 4,
         out_specs=[pl.BlockSpec(memory_space=pltpu.VMEM)] * 2,
         scratch_shapes=[
+            *(pltpu.VMEM(a.shape, a.dtype) for a in (data, tile, cell, comp)),
             rows(),
             rows(),
             rows(),
             rows(),
+            pltpu.SemaphoreType.DMA((4,)),
             pltpu.SemaphoreType.DMA((ny - 1,)),
             pltpu.SemaphoreType.DMA((ny - 1,)),
             pltpu.SemaphoreType.DMA((nx - 1,)),
@@ -172,7 +192,7 @@
             collective_id=0, has_side_effects=True, vmem_limit_bytes=16 * MIB
         ),
         name="route",
-    )(data, tile, cell, comp)
+    )(*(pltpu.with_memory_space_constraint(a, pltpu.HBM) for a in (data, tile, cell, comp)))
 
 
 def scatter_kernel(cap, code_ref, got_ref, out_ref, quad, wide):
@@ -184,8 +204,9 @@
     codes = codes + pltpu.roll(codes, SPAN, 1)
     codes = codes + pltpu.roll(codes, 2 * SPAN, 1)
     total = got
-    for d in range(1, cap):
-        same = (codes == pltpu.roll(codes, d, 1)) & (slot >= d)
+    place_in_group = slot - slot // GROUP * GROUP
+    for d in range(1, GROUP):
+        same = (codes == pltpu.roll(codes, d, 1)) & (place_in_group >= d)
         total = total + jnp.where(same, pltpu.roll(got, d, 1), 0.0)
     for t in range(FIELDS):
         quad[pl.ds(t, devices, stride=FIELDS), :] = jnp.where(
@@ -213,18 +234,22 @@
     lax.fori_loop(0, rows // step, clear, 0)
     depth = lax.broadcasted_iota(jnp.int32, (FIELDS, LANES), 1)
 
-    def place(s, _):
-        where, news = [], []
-        for i in range(cap):
-            code = code_ref[s, (FIELDS - 1) * SPAN + i]
-            row = pl.ds(pl.multiple_of(lax.shift_right_logical(code, 7) * FIELDS, FIELDS), FIELDS)
-            news.append(out_ref[row, :] + wide[i, pl.ds(pl.multiple_of(s * FIELDS, FIELDS), FIELDS), :])
-            where.append((row, depth == jnp.bitwise_and(code, LANES - 1)))
-        for (row, mask), new in zip(where, news):
-            pltpu.store(out_ref.at[row, :], new, mask=mask)
+    def place(q, _):
+        for p in range(FIELDS):
+            s = q * FIELDS + p
+            for start in range(0, cap, GROUP):
+                where, news = [], []
+                for i in range(start, min(cap, start + GROUP)):
+                    word = code_ref[q, p * SPAN + i]
+                    row = pl.ds(pl.multiple_of(lax.shift_right_logical(word, 7), FIELDS), FIELDS)
+                    news.append(out_ref[row, :] + wide[i, pl.ds(pl.multiple_of(s * FIELDS, FIELDS), FIELDS), :])
+                    column = jnp.bitwise_and(jnp.full((FIELDS, LANES), word, jnp.int32), LANES - 1)
+                    where.append((row, depth == column))
+                for (row, mask), new in zip(where, news):
+                    pltpu.store(out_ref.at[row, :], new, mask=mask)
         return 0
 
-    lax.fori_loop(0, devices, place, 0)
+    lax.fori_loop(0, devices // FIELDS, place, 0)
 
 
 def scatter(cap, rows, codes, got):
@@ -238,7 +263,7 @@
             pltpu.VMEM((devices * FIELDS, LANES), jnp.float32),
             pltpu.VMEM((cap, devices * FIELDS, LANES), jnp.float32),
         ],
-        compiler_params=pltpu.CompilerParams(vmem_limit_bytes=32 * MIB),
+        compiler_params=pltpu.CompilerParams(vmem_limit_bytes=24 * MIB),
         name="scatter",
     )(codes, got)
 
@@ -250,15 +275,13 @@
     h_in,
     cond_in,
     perm_in,
-    fwd_in,
-    src_in,
+    fwd,
+    src,
     e,
     h,
     grad,
     decay,
     gain,
-    fwd,
-    src,
     ex_got,
     ey_got,
     hx_got,
@@ -267,7 +290,6 @@
     ey_put,
     hx_put,
     hy_put,
-    load,
     send,
     recv,
 ):
@@ -280,22 +302,6 @@
     for other in (below_x, above_x, below_y, above_y):
         pl.semaphore_signal(barrier, inc=1, device_id=other, device_id_type=MESH)
 
-    loads = [
-        pltpu.make_async_copy(a, b, load.at[n])
-        for n, (a, b) in enumerate(
-            (
-                (e_in, e),
-                (h_in, h),
-                (cond_in, decay),
-                (perm_in, gain),
-                (src_in, src),
-                (fwd_in, fwd),
-            )
-        )
-    ]
-    for copy in loads:
-        copy.start()
-
     size_x, size_y, depth = e.shape[1:]
     shape = (size_y, depth)
     row = lax.broadcasted_iota(jnp.int32, shape, 0)
@@ -324,15 +330,16 @@
         ey_put[t, 1, pl.ds(p, 1), :] = ez[:1]
 
     def h_plane(x, p, t, next_y, next_z):
-        ex, ey, ez = e[0, x], e[1, x], e[2, x]
+        es, hs = (e_in, h_in) if t == 0 else (e, h)
+        ex, ey, ez = es[0, x], es[1, x], es[2, x]
         after_x = ey_got[t, 0, pl.ds(p, 1), :] * keep_ey
         after_z = ey_got[t, 1, pl.ds(p, 1), :] * keep_ey
         curl_x = (up_y(ez, after_z) - ez) - (up_z(ey) - ey)
         curl_y = (up_z(ex) - ex) - (next_z - ez)
         curl_z = (next_y - ey) - (up_y(ex, after_x) - ex)
-        hx = h[0, x] - time_step * curl_x
-        hy = h[1, x] - time_step * curl_y
-        hz = h[2, x] - time_step * curl_z
+        hx = hs[0, x] - time_step * curl_x
+        hy = hs[1, x] - time_step * curl_y
+        hz = hs[2, x] - time_step * curl_z
         h[0, x] = hx
         h[1, x] = hy
         h[2, x] = hz
@@ -347,8 +354,8 @@
         curl_y = (hx - down_z(hx)) - (hz - last_z)
         curl_z = (hy - last_y) - (hx - down_y(hx, before_x))
         if t == 0:
-            half_loss = decay[x] * (0.5 * time_step)
-            eps = gain[x]
+            half_loss = cond_in[x] * (0.5 * time_step)
+            eps = perm_in[x]
             inverse = 1.0 / (eps + half_loss)
             fade = (eps - half_loss) * inverse
             rise = time_step * inverse
@@ -356,10 +363,11 @@
             gain[x] = rise
         else:
             fade, rise = decay[x], gain[x]
+        es = e_in if t == 0 else e
         total = None
         for c, curl in enumerate((curl_x, curl_y, curl_z)):
             source = src[c, x, pl.ds(t, size_y, stride=FIELDS), :]
-            new = fade * e[c, x] + rise * (curl - source)
+            new = fade * es[c, x] + rise * (curl - source)
             e[c, x] = new
             term = fwd[t, c, x].astype(jnp.float32) * new
             total = term if total is None else total + term
@@ -389,44 +397,38 @@
             remote(hx_put.at[t], hx_got.at[t], 4 * t + 3, above_x),
         )
 
-    loads[0].wait()
-
     def first_rows(p, _):
         x = lax.rem(p + 1, size_x)
-        e_rows(x, p, 0, e[0, x], e[2, x])
+        e_rows(x, p, 0, e_in[0, x], e_in[2, x])
         return 0
 
     lax.fori_loop(0, size_x, first_rows, 0)
     pl.semaphore_wait(barrier, 4)
     pending = []
     for t in range(STEPS):
-        ex_put[t, 0] = e[1, 0]
-        ex_put[t, 1] = e[2, 0]
+        es = e_in if t == 0 else e
+        ex_put[t, 0] = es[1, 0]
+        ex_put[t, 1] = es[2, 0]
         across, along = e_copies(t)
         across.start()
         along.start()
-        if t == 0:
-            loads[1].wait()
         across.wait_recv()
 
         def h_inner(p, _):
             x = p + 1
-            h_plane(x, p, t, e[1, x + 1], e[2, x + 1])
+            h_plane(x, p, t, es[1, x + 1], es[2, x + 1])
             return 0
 
         lax.fori_loop(0, size_x - 2, h_inner, 0)
         along.wait_recv()
         h_plane(size_x - 1, size_x - 2, t, ex_got[t, 0] * keep_ex, ex_got[t, 1] * keep_ex)
-        h_plane(0, size_x - 1, t, e[1, 1], e[2, 1])
+        h_plane(0, size_x - 1, t, es[1, 1], es[2, 1])
         pending += [across, along]
         hx_put[t, 0] = h[1, size_x - 1]
         hx_put[t, 1] = h[2, size_x - 1]
         across, along = h_copies(t)
         across.start()
         along.start()
-        if t == 0:
-            for n in (2, 3, 4, 5):
-                loads[n].wait()
         across.wait_recv()
 
         def e_inner(p, _):
@@ -452,13 +454,11 @@
     return pl.pallas_call(
         functools.partial(steps_kernel, nx, ny),
         out_shape=[field, field, single],
-        in_specs=[pl.BlockSpec(memory_space=pl.ANY)] * 6,
+        in_specs=[pl.BlockSpec(memory_space=pltpu.VMEM)] * 6,
         out_specs=[pl.BlockSpec(memory_space=pltpu.VMEM)] * 3,
         scratch_shapes=[
             whole(cond),
             whole(perm),
-            whole(fwd),
-            whole(src),
             x_halo(),
             y_halo(),
             x_halo(),
@@ -467,12 +467,11 @@
             y_halo(),
             x_halo(),
             y_halo(),
-            pltpu.SemaphoreType.DMA((6,)),
             pltpu.SemaphoreType.DMA((4 * STEPS,)),
             pltpu.SemaphoreType.DMA((4 * STEPS,)),
         ],
         compiler_params=pltpu.CompilerParams(
-            collective_id=1, has_side_effects=True, vmem_limit_bytes=40 * MIB
+            collective_id=1, has_side_effects=True, vmem_limit_bytes=8 * MIB
         ),
         name="steps",
     )(e, h, cond, perm, fwd, src)

time: 87.4 us -> 75.7 us (0.87)
  local copies, waits for them, and re-layouts: 9.56 us -> 3.41 us
  Pallas kernels: 76.9 us -> 71.4 us
    unnamed x23 -> x13, local copies, waits for them, and re-layouts: 9.56 us -> 3.41 us
    pallas_call x1, Pallas kernels: 13.3 us -> 7.42 us  [scatter(): pl.pallas_call(functools.partial(scatter_kernel, cap), out_shape=jax.Shap...]
    pallas_call x1, Pallas kernels: 16.1 us -> 17.3 us  [route(): pl.pallas_call(functools.partial(route_kernel, nx, ny, cells), out_shape=...]
where the time goes in v1:
time: 75.7 us; the launch traced here: 75.5 us
  Pallas kernels  71.4 us (94%)
  local copies, waits for them, and re-layouts  3.41 us (5%)
    pallas_call x1, Pallas kernels, steps(): pl.pallas_call(functools.partial(steps_kernel, nx, ny), out_shape=[field,...  46.6 us
    pallas_call x1, Pallas kernels, route(): pl.pallas_call(functools.partial(route_kernel, nx, ny, cells), out_shape=...  17.3 us
    pallas_call x1, Pallas kernels, scatter(): pl.pallas_call(functools.partial(scatter_kernel, cap), out_shape=jax.Shap...  7.42 us
    unnamed x13, local copies, waits for them, and re-layouts  3.41 us

profile of v1, /device:TPU:0, one launch (start us, length us, event | category | flops | bytes accessed | tf_op | source)
XLA Modules:
  0.0 75.5 jit_solution(4782136980314605184)
XLA Ops:
  0.6 0.0 copy-start.4
  0.6 17.3 %route.1 = (f32[128,128]{1,0:T(8,128)S(1)}, s32[32,128]{1,0:T(8,128)S(1)}) custom-call(f32[1024,128]{1,0:T(8,128)} %data_in.1, s32[8,128]{1,0:T(8,128)} %bitcast.5, s32[8,128]{1,0:T(8,128)} %bitcast.6, s32[8,128]{1,0:T(8,128)} %bitcast.7), custom_call_target="tpu_custom_call" | custom-call | tf_op jit(solution)/shard_map/route/pallas_call | solution.py:171
  18.0 0.0 copy-start
  18.0 0.0 copy-start.1
  18.0 0.0 copy-start.2
  18.0 0.0 copy-start.3
  18.0 7.4 %scatter.1 = f32[15360,128]{1,0:T(8,128)S(1)} custom-call(s32[32,128]{1,0:T(8,128)S(1)} %get-tuple-element.5.code_ref, f32[128,128]{1,0:T(8,128)S(1)} %get-tuple-element.6.got_ref), custom_call_target="tpu_custom_call" | custom-call | tf_op jit(solution)/shard_map/scatter/pallas_call | solution.py:257
  25.5 0.0 copy-done.4
  25.5 0.0 copy-done
  25.5 0.0 copy-done.1
  25.5 0.0 copy-done.2
  25.5 0.0 copy-done.3
  25.5 46.6 %steps.1 = (f32[3,32,40,128]{3,2,1,0:T(8,128)S(1)}, f32[3,32,40,128]{3,2,1,0:T(8,128)S(1)}, f32[32,40,128]{2,1,0:T(8,128)S(1)}) custom-call(f32[3,32,40,128]{3,2,1,0:T(8,128)S(1)} %copy-done.1, f32[3,32,40,128]{3,2,1,0:T(8,128)S(1)} %copy-done.2, f32[32,40,128]{2,1,0:T(8,128)S(1)} %copy-done.3, f32[32,40,128]{2,1,0:T(8,128)S(1)} %copy-done.4, ...), custom_call_target="tpu_custom_call" | custom-call | tf_op jit(solution)/shard_map/steps/pallas_call | solution.py:454
  72.2 1.3 %copy.15 = f32[3,32,40,128]{3,2,1,0:T(8,128)} copy(f32[3,32,40,128]{3,2,1,0:T(8,128)S(1)} %get-tuple-element.10) | data formatting | bytes 3932160
  73.4 1.3 %copy.16 = f32[3,32,40,128]{3,2,1,0:T(8,128)} copy(f32[3,32,40,128]{3,2,1,0:T(8,128)S(1)} %get-tuple-element.11) | data formatting | bytes 3932160
  74.7 0.8 %copy.17 = f32[32,40,128]{2,1,0:T(8,128)} copy(f32[32,40,128]{2,1,0:T(8,128)S(1)} %get-tuple-element.12) | data formatting | bytes 1310720
Async XLA Ops:
  0.6 24.8 %copy-start.4 = (f32[32,40,128]{2,1,0:T(8,128)S(1)}, f32[32,40,128]{2,1,0:T(8,128)}, u32[]{:S(2)}) copy-start(f32[32,40,128]{2,1,0:T(8,128)} %perm_in.1) | copy-start | bytes 1966084
  18.0 7.5 %copy-start = (bf16[3,3,32,40,128]{4,3,2,1,0:T(8,128)(2,1)S(1)}, bf16[3,3,32,40,128]{4,3,2,1,0:T(8,128)(2,1)}, u32[]{:S(2)}) copy-start(bf16[3,3,32,40,128]{4,3,2,1,0:T(8,128)(2,1)} %fwd.1) | copy-start | bytes 8847364
  18.0 7.5 %copy-start.1 = (f32[3,32,40,128]{3,2,1,0:T(8,128)S(1)}, f32[3,32,40,128]{3,2,1,0:T(8,128)}, u32[]{:S(2)}) copy-start(f32[3,32,40,128]{3,2,1,0:T(8,128)} %e_in.1) | copy-start | bytes 5898244
  18.0 7.5 %copy-start.2 = (f32[3,32,40,128]{3,2,1,0:T(8,128)S(1)}, f32[3,32,40,128]{3,2,1,0:T(8,128)}, u32[]{:S(2)}) copy-start(f32[3,32,40,128]{3,2,1,0:T(8,128)} %h_in.1) | copy-start | bytes 5898244
  18.0 7.5 %copy-start.3 = (f32[32,40,128]{2,1,0:T(8,128)S(1)}, f32[32,40,128]{2,1,0:T(8,128)}, u32[]{:S(2)}) copy-start(f32[32,40,128]{2,1,0:T(8,128)} %cond_in.1) | copy-start | bytes 1966084

commit v2 on v1

v2 whole, which is shorter than its diff:
```python
import functools

import jax
import jax.numpy as jnp
from jax import lax
from jax.experimental import pallas as pl
from jax.experimental.pallas import tpu as pltpu
from jax.sharding import PartitionSpec as P

STEPS = 3
SAMPLES = 128
LANES = 128
FIELDS = 4
SPAN = LANES // FIELDS
MESH = pl.DeviceIdType.MESH
GROUP = 12
MIB = 1 << 20

time_step = 0.55


def split3(x):
    a = x.astype(jnp.bfloat16)
    rest = x - a.astype(jnp.float32)
    b = rest.astype(jnp.bfloat16)
    c = (rest - b.astype(jnp.float32)).astype(jnp.bfloat16)
    return a, b, c


def mm(a, b, contract=((1,), (0,))):
    return lax.dot_general(a, b, (contract, ((), ())), preferred_element_type=jnp.float32)


def time_kernel():
    rows = 8
    sample = lax.broadcasted_iota(jnp.int32, (rows, SAMPLES), 1).astype(jnp.float32)
    step = lax.broadcasted_iota(jnp.int32, (rows, SAMPLES), 0).astype(jnp.float32)
    centre = (step + 0.5) * (SAMPLES / STEPS)
    spread = SAMPLES / (4.0 * STEPS)
    kernel = jnp.exp(-jnp.square((sample - centre) / spread))
    kernel = jnp.where(step < STEPS - 0.5, kernel, 0.0)
    norm = jnp.sum(kernel * kernel, axis=1, keepdims=True)
    return kernel / jnp.sqrt(jnp.where(norm > 0.0, norm, 1.0))


def pack(devices, cells, data_ref, tile_ref, cell_ref, comp_ref):
    blocks, width = tile_ref.shape
    kernel = time_kernel()
    before = (
        lax.broadcasted_iota(jnp.int32, (width, width), 0)
        < lax.broadcasted_iota(jnp.int32, (width, width), 1)
    ).astype(jnp.bfloat16)
    every = jnp.ones((width, width), jnp.bfloat16)
    destination = lax.broadcasted_iota(jnp.int32, (devices, width), 0)
    slot = lax.broadcasted_iota(jnp.int32, (SPAN, width), 0).astype(jnp.float32)
    seen = jnp.zeros((devices, width), jnp.float32)
    packed = jnp.zeros((devices, LANES), jnp.float32)
    for b in range(blocks):
        onehot = (destination == tile_ref[b : b + 1, :]).astype(jnp.float32)
        hot = onehot.astype(jnp.bfloat16)
        rank = jnp.sum(onehot * (seen + mm(hot, before)), axis=0, keepdims=True)
        seen = seen + mm(hot, every)
        amplitude = lax.dot_general(
            kernel,
            data_ref[b * width : (b + 1) * width, :],
            (((1,), (1,)), ((), ())),
            precision=lax.Precision.HIGHEST,
            preferred_element_type=jnp.float32,
        )
        code = (comp_ref[b : b + 1, :] * cells + cell_ref[b : b + 1, :]).astype(jnp.float32)
        here = slot == rank
        fields = [amplitude[t : t + 1, :] for t in range(STEPS)] + [code]
        spread = jnp.concatenate([jnp.where(here, f, 0.0) for f in fields], axis=0)
        for term in split3(spread):
            packed = packed + mm(hot, term, ((1,), (1,)))
    return packed


class Place:
    def __init__(self, nx, ny):
        self.nx, self.ny = nx, ny
        self.ix, self.iy = lax.axis_index("gx"), lax.axis_index("gy")
        self.lo_x, self.hi_x = lax.rem(self.ix + nx - 1, nx), lax.rem(self.ix + 1, nx)
        self.lo_y, self.hi_y = lax.rem(self.iy + ny - 1, ny), lax.rem(self.iy + 1, ny)
        one, zero = jnp.float32(1.0), jnp.float32(0.0)
        self.keep_lo_x = jnp.where(self.ix == 0, zero, one)
        self.keep_hi_x = jnp.where(self.ix == nx - 1, zero, one)
        self.keep_lo_y = jnp.where(self.iy == 0, zero, one)
        self.keep_hi_y = jnp.where(self.iy == ny - 1, zero, one)

    def corners(self):
        return [(x, y) for x in (self.lo_x, self.hi_x) for y in (self.lo_y, self.hi_y)]

    def sides(self):
        return [(self.lo_x, self.iy), (self.hi_x, self.iy), (self.ix, self.lo_y), (self.ix, self.hi_y)]

    def plane(self, p, size_x):
        return jnp.where(p < 2, self.keep_lo_x, jnp.where(p >= size_x + 2, self.keep_hi_x, 1.0))


def shifts(rows, depth):
    lane = lax.broadcasted_iota(jnp.int32, (rows, depth), 1)

    def up_z(f):
        return jnp.where(lane == depth - 1, 0.0, pltpu.roll(f, depth - 1, 1))

    def down_z(f):
        return jnp.where(lane == 0, 0.0, pltpu.roll(f, 1, 1))

    def up_y(f):
        return pltpu.roll(f, rows - 1, 0)

    def down_y(f):
        return pltpu.roll(f, 1, 0)

    return up_z, down_z, up_y, down_y


def h_plane(e, h_from, h_to, p, factor, moves):
    up_z, _, up_y, _ = moves
    ex, ey, ez = e[0, p], e[1, p], e[2, p]
    curl_x = (up_y(ez) - ez) - (up_z(ey) - ey)
    curl_y = (up_z(ex) - ex) - (e[2, p + 1] - ez)
    curl_z = (e[1, p + 1] - ey) - (up_y(ex) - ex)
    for c, curl in enumerate((curl_x, curl_y, curl_z)):
        h_to[c, p] = h_from[c, p] - factor * curl


def curl_h(h, p, moves):
    _, down_z, _, down_y = moves
    hx, hy, hz = h[0, p], h[1, p], h[2, p]
    curl_x = (hz - down_y(hz)) - (hy - down_z(hy))
    curl_y = (hx - down_z(hx)) - (hz - h[2, p - 1])
    curl_z = (hy - h[1, p - 1]) - (hx - down_y(hx))
    return curl_x, curl_y, curl_z


def h_factor(place, size_y, rows, depth):
    row = lax.broadcasted_iota(jnp.int32, (rows, depth), 0)
    beyond = jnp.where(row < size_y + 4, place.keep_hi_y, place.keep_lo_y)
    return time_step * jnp.where(row < size_y, 1.0, beyond)


def row_copies(dn_put, up_put, up_got, lo_got, size_x, place):
    first, last, low, high = pl.ds(0, 2), pl.ds(size_x - 2, 2), pl.ds(0, 2), pl.ds(size_x + 2, 2)
    whole = pl.ds(2, size_x)
    return [
        (dn_put, up_got.at[:, whole], (place.ix, place.lo_y)),
        (up_put, lo_got.at[:, whole], (place.ix, place.hi_y)),
        (dn_put.at[:, first], up_got.at[:, high], (place.lo_x, place.lo_y)),
        (dn_put.at[:, last], up_got.at[:, low], (place.hi_x, place.lo_y)),
        (up_put.at[:, first], lo_got.at[:, high], (place.lo_x, place.hi_y)),
        (up_put.at[:, last], lo_got.at[:, low], (place.hi_x, place.hi_y)),
    ]


def plane_copies(array, count, size_x, size_y, place):
    lead = (slice(None),) * (len(array.shape) - 3)
    rows = pl.ds(0, size_y)

    def part(start):
        return array.at[(*lead, pl.ds(start, count), rows)]

    return [
        (part(2), part(size_x + 2), (place.lo_x, place.iy)),
        (part(size_x + 2 - count), part(2 - count), (place.hi_x, place.iy)),
    ]


def start_copies(parts, send, recv):
    copies = [
        pltpu.make_async_remote_copy(
            src_ref=a,
            dst_ref=b,
            send_sem=send.at[n],
            recv_sem=recv.at[n],
            device_id=device,
            device_id_type=MESH,
        )
        for n, (a, b, device) in enumerate(parts)
    ]
    for copy in copies:
        copy.start()
    return copies


def route_kernel(
    nx,
    ny,
    cells,
    data_in,
    tile_in,
    cell_in,
    comp_in,
    e_in,
    h_in,
    cond_in,
    perm_in,
    got_ref,
    code_ref,
    h,
    base,
    decay,
    gain,
    data_ref,
    tile_ref,
    cell_ref,
    comp_ref,
    e,
    first,
    mid,
    second,
    last,
    dn_put,
    up_put,
    up_got,
    lo_got,
    load,
    send_y,
    recv_y,
    send_x,
    recv_x,
    send,
    recv,
):
    place = Place(nx, ny)
    ix, iy = place.ix, place.iy
    size_x, size_y, depth = base.shape[1:]
    rows = size_y + 8
    inner = (pl.ds(2, size_x), pl.ds(0, size_y))
    pairs = (
        (tile_in, tile_ref),
        (cell_in, cell_ref),
        (comp_in, comp_ref),
        (data_in, data_ref),
        (e_in, e.at[:, inner[0], inner[1]]),
        (h_in, h.at[:, inner[0], inner[1]]),
        (cond_in, decay.at[inner[0], inner[1]]),
        (perm_in, gain.at[inner[0], inner[1]]),
    )
    loads = [pltpu.make_async_copy(a, b, load.at[n]) for n, (a, b) in enumerate(pairs)]
    for copy in loads:
        copy.start()
    barrier = pltpu.get_barrier_semaphore()
    for k in range(1, nx):
        pl.semaphore_signal(barrier, inc=1, device_id=(lax.rem(ix + k, nx), iy), device_id_type=MESH)
    for k in range(1, ny):
        pl.semaphore_signal(barrier, inc=1, device_id=(ix, lax.rem(iy + k, ny)), device_id_type=MESH)
    for other in place.corners():
        pl.semaphore_signal(barrier, inc=1, device_id=other, device_id_type=MESH)
    for copy in loads:
        copy.wait()

    def stage(x, _):
        p = x + 2
        n = 0
        for array in (e, h):
            for c in range(3):
                for r in range(2):
                    dn_put[n, x] = array[c, p, r : r + 1, :]
                    up_put[n, x] = array[c, p, size_y - 2 + r : size_y - 1 + r, :]
                    n += 1
        for array in (decay, gain):
            dn_put[n, x] = array[p, 0:1, :]
            up_put[n, x] = array[p, size_y - 1 : size_y, :]
            n += 1
        return 0

    lax.fori_loop(0, size_x, stage, 0)
    pl.semaphore_wait(barrier, nx + ny + 2)
    halos = start_copies(
        row_copies(dn_put, up_put, up_got, lo_got, size_x, place)
        + plane_copies(e, 2, size_x, size_y, place)
        + plane_copies(h, 2, size_x, size_y, place)
        + plane_copies(decay, 1, size_x, size_y, place)
        + plane_copies(gain, 1, size_x, size_y, place),
        send,
        recv,
    )
    first[...] = pack(nx * ny, cells, data_ref, tile_ref, cell_ref, comp_ref)

    copies = []
    for k in range(1, nx):
        to = lax.rem(ix + k, nx)
        copy = pltpu.make_async_remote_copy(
            src_ref=first.at[pl.ds(pl.multiple_of(to * ny, ny), ny), :],
            dst_ref=mid.at[pl.ds(pl.multiple_of(ix * ny, ny), ny), :],
            send_sem=send_x.at[k - 1],
            recv_sem=recv_x.at[k - 1],
            device_id=(to, iy),
            device_id_type=MESH,
        )
        copy.start()
        copies.append(copy)
    own = pl.ds(pl.multiple_of(ix * ny, ny), ny)
    mid[own, :] = first[own, :]
    for copy in copies:
        copy.wait_recv()
    for j in range(ny):
        second[j * nx : (j + 1) * nx, :] = mid[pl.ds(j, nx, stride=ny), :]
    later = []
    for k in range(1, ny):
        to = lax.rem(iy + k, ny)
        copy = pltpu.make_async_remote_copy(
            src_ref=second.at[pl.ds(pl.multiple_of(to * nx, nx), nx), :],
            dst_ref=last.at[pl.ds(pl.multiple_of(iy * nx, nx), nx), :],
            send_sem=send_y.at[k - 1],
            recv_sem=recv_y.at[k - 1],
            device_id=(ix, to),
            device_id_type=MESH,
        )
        copy.start()
        later.append(copy)
    own = pl.ds(pl.multiple_of(iy * nx, nx), nx)
    last[own, :] = second[own, :]
    for copy in copies:
        copy.wait_send()

    for copy in halos:
        copy.wait()
    for p in (0, 1, size_x + 2, size_x + 3):
        keep = place.plane(p, size_x)
        for c in range(3):
            for array in (e, h):
                array[c, p, :size_y] = array[c, p, :size_y] * keep

    def unstage(p, _):
        keep = place.plane(p, size_x)
        above, below = keep * place.keep_hi_y, keep * place.keep_lo_y
        n = 0
        gap = jnp.zeros((4, depth), jnp.float32)
        for array in (e, h):
            for c in range(3):
                array[c, p, size_y:] = jnp.concatenate(
                    [up_got[n, p] * above, up_got[n + 1, p] * above, gap, lo_got[n, p] * below, lo_got[n + 1, p] * below],
                    axis=0,
                )
                n += 2
        return 0

    lax.fori_loop(0, size_x + 4, unstage, 0)
    row = lax.broadcasted_iota(jnp.int32, (rows, depth), 0)
    inside = jnp.where(
        row < size_y,
        1.0,
        jnp.where(row == size_y, place.keep_hi_y, jnp.where(row == rows - 1, place.keep_lo_y, 0.0)),
    )
    ones = jnp.ones((6, depth), jnp.float32)

    def coefficients(p, _):
        decay[p, size_y:] = jnp.concatenate([up_got[12, p], ones, lo_got[12, p]], axis=0)
        gain[p, size_y:] = jnp.concatenate([up_got[13, p], ones, lo_got[13, p]], axis=0)
        half_loss = decay[p] * (0.5 * time_step)
        eps = gain[p]
        inverse = 1.0 / (eps + half_loss)
        keep = inside * place.plane(p, size_x)
        decay[p] = (eps - half_loss) * inverse * keep
        gain[p] = time_step * inverse * keep
        return 0

    lax.fori_loop(1, size_x + 3, coefficients, 0)
    moves = shifts(rows, depth)
    factor = h_factor(place, size_y, rows, depth)

    def h_step(p, _):
        h_plane(e, h, h, p, factor * place.plane(p, size_x), moves)
        return 0

    lax.fori_loop(0, size_x + 3, h_step, 0)

    def e_step(x, _):
        p = x + 2
        for c, curl in enumerate(curl_h(h, p, moves)):
            new = decay[p] * e[c, p] + gain[p] * curl
            base[c, x] = new[:size_y]
        return 0

    lax.fori_loop(0, size_x, e_step, 0)

    for copy in later:
        copy.wait()
    got_ref[...] = last[...]
    quarter = nx * ny // FIELDS
    lane = lax.broadcasted_iota(jnp.int32, (quarter, LANES), 1) // SPAN
    codes = jnp.zeros((quarter, LANES), jnp.int32)
    for k in range(FIELDS):
        code = last[pl.ds(k, quarter, stride=FIELDS), :].astype(jnp.int32)
        word = jnp.bitwise_and(code, LANES - 1) + jnp.bitwise_and(code, -LANES) * FIELDS
        codes = jnp.where(lane == k, pltpu.roll(word, (k + 1) * SPAN % LANES, 1), codes)
    code_ref[...] = codes


def in_vmem(count):
    return [pl.BlockSpec(memory_space=pltpu.VMEM)] * count


def f32(*shape):
    return jax.ShapeDtypeStruct(shape, jnp.float32)


def route(nx, ny, data, tile, cell, comp, e, h, cond, perm):
    devices = nx * ny
    size_x, size_y, depth = cond.shape
    wide, tall = size_x + 4, size_y + 8
    inputs = (data, tile, cell, comp, e, h, cond, perm)
    rows = lambda: pltpu.VMEM((devices, LANES), jnp.float32)
    count = 14
    return pl.pallas_call(
        functools.partial(route_kernel, nx, ny, size_x * size_y * depth),
        out_shape=[
            f32(devices, LANES),
            jax.ShapeDtypeStruct((devices // FIELDS, LANES), jnp.int32),
            f32(3, wide, tall, depth),
            f32(3, size_x, size_y, depth),
            f32(wide, tall, depth),
            f32(wide, tall, depth),
        ],
        in_specs=[pl.BlockSpec(memory_space=pltpu.HBM)] * 8,
        out_specs=in_vmem(6),
        scratch_shapes=[
            *(pltpu.VMEM(a.shape, a.dtype) for a in (data, tile, cell, comp)),
            pltpu.VMEM((3, wide, tall, depth), jnp.float32),
            rows(),
            rows(),
            rows(),
            rows(),
            pltpu.VMEM((count, size_x, 1, depth), jnp.float32),
            pltpu.VMEM((count, size_x, 1, depth), jnp.float32),
            pltpu.VMEM((count, wide, 1, depth), jnp.float32),
            pltpu.VMEM((count, wide, 1, depth), jnp.float32),
            pltpu.SemaphoreType.DMA((8,)),
            pltpu.SemaphoreType.DMA((ny - 1,)),
            pltpu.SemaphoreType.DMA((ny - 1,)),
            pltpu.SemaphoreType.DMA((nx - 1,)),
            pltpu.SemaphoreType.DMA((nx - 1,)),
            pltpu.SemaphoreType.DMA((14,)),
            pltpu.SemaphoreType.DMA((14,)),
        ],
        compiler_params=pltpu.CompilerParams(
            collective_id=0, has_side_effects=True, vmem_limit_bytes=16 * MIB
        ),
        name="route",
    )(*(pltpu.with_memory_space_constraint(a, pltpu.HBM) for a in inputs))


def scatter_kernel(cap, code_ref, got_ref, out_ref, quad, wide):
    devices = got_ref.shape[0]
    got = got_ref[...]
    lane = lax.broadcasted_iota(jnp.int32, (devices, LANES), 1)
    slot = jnp.bitwise_and(lane, SPAN - 1)
    codes = jnp.where(lane >= (FIELDS - 1) * SPAN, got, 0.0)
    codes = codes + pltpu.roll(codes, SPAN, 1)
    codes = codes + pltpu.roll(codes, 2 * SPAN, 1)
    total = got
    place_in_group = slot - slot // GROUP * GROUP
    for d in range(1, GROUP):
        same = (codes == pltpu.roll(codes, d, 1)) & (place_in_group >= d)
        total = total + jnp.where(same, pltpu.roll(got, d, 1), 0.0)
    for t in range(FIELDS):
        quad[pl.ds(t, devices, stride=FIELDS), :] = jnp.where(
            (lane >= t * SPAN) & (lane < (t + 1) * SPAN), total, 0.0
        )
    values = quad[...]
    high = values.astype(jnp.bfloat16)
    low = (values - high.astype(jnp.float32)).astype(jnp.bfloat16)
    terms = jnp.concatenate([high, low], axis=1)
    row_slot = jnp.bitwise_and(lax.broadcasted_iota(jnp.int32, (2 * LANES, 2 * LANES), 0), SPAN - 1)
    column = lax.broadcasted_iota(jnp.int32, (2 * LANES, 2 * LANES), 1) // LANES
    for i in range(0, cap, 2):
        pick = (row_slot == column + i).astype(jnp.bfloat16)
        both = mm(terms, pick)
        wide[i] = both[:, :LANES]
        wide[i + 1] = both[:, LANES:]

    rows = out_ref.shape[0]
    step = 128

    def clear(n, _):
        out_ref[pl.ds(pl.multiple_of(n * step, step), step), :] = jnp.zeros((step, LANES), jnp.float32)
        return 0

    lax.fori_loop(0, rows // step, clear, 0)
    depth = lax.broadcasted_iota(jnp.int32, (FIELDS, LANES), 1)

    def place(q, _):
        for p in range(FIELDS):
            s = q * FIELDS + p
            for start in range(0, cap, GROUP):
                where, news = [], []
                for i in range(start, min(cap, start + GROUP)):
                    word = code_ref[q, p * SPAN + i]
                    row = pl.ds(pl.multiple_of(lax.shift_right_logical(word, 7), FIELDS), FIELDS)
                    news.append(out_ref[row, :] + wide[i, pl.ds(pl.multiple_of(s * FIELDS, FIELDS), FIELDS), :])
                    column = jnp.bitwise_and(jnp.full((FIELDS, LANES), word, jnp.int32), LANES - 1)
                    where.append((row, depth == column))
                for (row, mask), new in zip(where, news):
                    pltpu.store(out_ref.at[row, :], new, mask=mask)
        return 0

    lax.fori_loop(0, devices // FIELDS, place, 0)


def scatter(cap, rows, codes, got):
    devices = got.shape[0]
    return pl.pallas_call(
        functools.partial(scatter_kernel, cap),
        out_shape=jax.ShapeDtypeStruct((rows * FIELDS, LANES), jnp.float32),
        in_specs=[pl.BlockSpec(memory_space=pltpu.SMEM), pl.BlockSpec(memory_space=pltpu.VMEM)],
        out_specs=pl.BlockSpec(memory_space=pltpu.VMEM),
        scratch_shapes=[
            pltpu.VMEM((devices * FIELDS, LANES), jnp.float32),
            pltpu.VMEM((cap, devices * FIELDS, LANES), jnp.float32),
        ],
        compiler_params=pltpu.CompilerParams(vmem_limit_bytes=24 * MIB),
        name="scatter",
    )(codes, got)


def share_kernel(
    nx, ny, base, gain, src, fwd, e, src1, grad, dn_put, up_put, up_got, lo_got, send, recv
):
    place = Place(nx, ny)
    size_x, size_y, depth = base.shape[1:]
    barrier = pltpu.get_barrier_semaphore()
    others = place.sides() + place.corners()
    for other in others:
        pl.semaphore_signal(barrier, inc=1, device_id=other, device_id_type=MESH)

    def own(x, _):
        p = x + 2
        rise = gain[p, :size_y]
        for c in range(3):
            new = base[c, x] - rise * src[c, x, pl.ds(0, size_y, stride=FIELDS), :]
            e[c, p, :size_y] = new
            source = src[c, x, pl.ds(1, size_y, stride=FIELDS), :]
            src1[c, p, :size_y] = source
            for r in range(2):
                dn_put[2 * c + r, x] = new[r : r + 1]
                up_put[2 * c + r, x] = new[size_y - 2 + r : size_y - 1 + r]
            dn_put[6 + c, x] = source[:1]
            up_put[6 + c, x] = source[size_y - 1 :]
        return 0

    lax.fori_loop(0, size_x, own, 0)
    pl.semaphore_wait(barrier, len(others))
    copies = start_copies(
        row_copies(dn_put, up_put, up_got, lo_got, size_x, place)
        + plane_copies(e, 2, size_x, size_y, place)
        + plane_copies(src1, 1, size_x, size_y, place),
        send,
        recv,
    )

    def product(x, _):
        total = fwd[0, 0, x].astype(jnp.float32) * e[0, x + 2, :size_y]
        for c in (1, 2):
            total = total + fwd[0, c, x].astype(jnp.float32) * e[c, x + 2, :size_y]
        grad[x] = total
        return 0

    lax.fori_loop(0, size_x, product, 0)
    for copy in copies:
        copy.wait()
    for p in (0, 1, size_x + 2, size_x + 3):
        keep = place.plane(p, size_x)
        for c in range(3):
            e[c, p, :size_y] = e[c, p, :size_y] * keep

    def unstage(p, _):
        keep = place.plane(p, size_x)
        above, below = keep * place.keep_hi_y, keep * place.keep_lo_y
        gap = jnp.zeros((4, depth), jnp.float32)
        for c in range(3):
            n = 2 * c
            e[c, p, size_y:] = jnp.concatenate(
                [up_got[n, p] * above, up_got[n + 1, p] * above, gap, lo_got[n, p] * below, lo_got[n + 1, p] * below],
                axis=0,
            )
            src1[c, p, size_y:] = jnp.concatenate([up_got[6 + c, p], gap, gap[:2], lo_got[6 + c, p]], axis=0)
        return 0

    lax.fori_loop(0, size_x + 4, unstage, 0)


def share(nx, ny, base, gain, src, fwd):
    size_x, size_y, depth = base.shape[1:]
    wide, tall = size_x + 4, size_y + 8
    count = 9
    return pl.pallas_call(
        functools.partial(share_kernel, nx, ny),
        out_shape=[f32(3, wide, tall, depth), f32(3, wide, tall, depth), f32(size_x, size_y, depth)],
        in_specs=in_vmem(4),
        out_specs=in_vmem(3),
        scratch_shapes=[
            pltpu.VMEM((count, size_x, 1, depth), jnp.float32),
            pltpu.VMEM((count, size_x, 1, depth), jnp.float32),
            pltpu.VMEM((count, wide, 1, depth), jnp.float32),
            pltpu.VMEM((count, wide, 1, depth), jnp.float32),
            pltpu.SemaphoreType.DMA((10,)),
            pltpu.SemaphoreType.DMA((10,)),
        ],
        compiler_params=pltpu.CompilerParams(
            collective_id=1, has_side_effects=True, vmem_limit_bytes=6 * MIB
        ),
        name="share",
    )(base, gain, src, fwd)


def finish_kernel(
    nx, ny, e1, h1, decay, gain, src1, src, fwd, grad1, e_out, h_out, grad_out, e, h, grad, sem
):
    place = Place(nx, ny)
    size_x, size_y, depth = grad1.shape
    rows = size_y + 8
    moves = shifts(rows, depth)
    factor = h_factor(place, size_y, rows, depth)

    def h_second(p, _):
        h_plane(e1, h1, h, p, factor * place.plane(p, size_x), moves)
        return 0

    lax.fori_loop(0, size_x + 3, h_second, 0)

    def e_second(p, inner):
        fade, rise = decay[p], gain[p]
        total = None
        for c, curl in enumerate(curl_h(h, p, moves)):
            new = fade * e1[c, p] + rise * (curl - src1[c, p])
            e[c, p] = new
            if inner:
                term = fwd[1, c, p - 2].astype(jnp.float32) * new[:size_y]
                total = term if total is None else total + term
        if inner:
            grad[p - 2] = grad1[p - 2] + total

    e_second(1, False)

    def e_inner(x, _):
        e_second(x + 2, True)
        return 0

    lax.fori_loop(0, size_x, e_inner, 0)
    e_second(size_x + 2, False)

    def h_third(p, _):
        h_plane(e, h, h, p, factor * place.plane(p, size_x), moves)
        return 0

    lax.fori_loop(1, size_x + 2, h_third, 0)
    inside = pl.ds(0, size_y)
    outs = [pltpu.make_async_copy(h.at[:, pl.ds(2, size_x), inside], h_out, sem.at[0])]
    outs[0].start()

    def e_third(x, _):
        p = x + 2
        fade, rise = decay[p, :size_y], gain[p, :size_y]
        total = grad[x]
        for c, curl in enumerate(curl_h(h, p, moves)):
            source = src[c, x, pl.ds(2, size_y, stride=FIELDS), :]
            new = fade * e[c, p, :size_y] + rise * (curl[:size_y] - source)
            e[c, p, :size_y] = new
            total = total + fwd[2, c, x].astype(jnp.float32) * new
        grad[x] = total
        return 0

    parts = 4
    each = size_x // parts
    for k in range(parts):
        lax.fori_loop(k * each, (k + 1) * each, e_third, 0)
        here = pl.ds(k * each, each)
        outs.append(
            pltpu.make_async_copy(
                e.at[:, pl.ds(2 + k * each, each), inside], e_out.at[:, here], sem.at[1 + 2 * k]
            )
        )
        outs.append(pltpu.make_async_copy(grad.at[here], grad_out.at[here], sem.at[2 + 2 * k]))
        outs[-2].start()
        outs[-1].start()
    for copy in outs:
        copy.wait()


def finish(nx, ny, e1, h1, decay, gain, src1, src, fwd, grad1):
    size_x, size_y, depth = grad1.shape
    field = f32(3, size_x, size_y, depth)
    return pl.pallas_call(
        functools.partial(finish_kernel, nx, ny),
        out_shape=[field, field, f32(size_x, size_y, depth)],
        in_specs=in_vmem(8),
        out_specs=[pl.BlockSpec(memory_space=pltpu.HBM)] * 3,
        scratch_shapes=[
            pltpu.VMEM(e1.shape, jnp.float32),
            pltpu.VMEM(h1.shape, jnp.float32),
            pltpu.VMEM(grad1.shape, jnp.float32),
            pltpu.SemaphoreType.DMA((9,)),
        ],
        compiler_params=pltpu.CompilerParams(vmem_limit_bytes=10 * MIB),
        name="finish",
    )(e1, h1, decay, gain, src1, src, fwd, grad1)


def per_device(
    e_adjoint,
    h_adjoint,
    conductivity,
    permittivity,
    forward_e,
    receiver_data,
    receiver_tile,
    receiver_cell,
    receiver_comp,
):
    _, size_x, size_y, depth = e_adjoint.shape
    nx, ny = lax.axis_size("gx"), lax.axis_size("gy")
    receivers = receiver_data.shape[0]
    cap = 3 * receivers // (nx * ny)
    by_lane = lambda a: a.reshape(receivers // LANES, LANES)
    got, codes, h1, base, decay, gain = route(
        nx,
        ny,
        receiver_data,
        by_lane(receiver_tile),
        by_lane(receiver_cell),
        by_lane(receiver_comp),
        e_adjoint,
        h_adjoint,
        conductivity,
        permittivity,
    )
    placed = scatter(cap, 3 * size_x * size_y, codes, got)
    placed = placed.reshape(3, size_x, size_y * FIELDS, depth)
    e1, src1, grad1 = share(nx, ny, base, gain, placed, forward_e)
    return tuple(finish(nx, ny, e1, h1, decay, gain, src1, placed, forward_e, grad1))


def solution(mesh):
    placed = (
        P(None, "gx", "gy", None),
        P(None, "gx", "gy", None),
        P("gx", "gy", None),
        P("gx", "gy", None),
        P(None, None, "gx", "gy", None),
        P(("gx", "gy"), None),
        P(("gx", "gy"), None),
        P(("gx", "gy")),
        P(("gx", "gy")),
    )
    return jax.shard_map(
        per_device,
        mesh=mesh,
        in_specs=placed,
        out_specs=(P(None, "gx", "gy", None), P(None, "gx", "gy", None), P("gx", "gy", None)),
        check_vma=False,
    )
```

time: 75.7 us -> 58.5 us (0.77)
  Pallas kernels: 71.4 us -> 57.7 us
  local copies, waits for them, and re-layouts: 3.41 us -> 0.01 us
    pallas_call x2 -> x3, Pallas kernels: 64 us -> 50.2 us  [the longest x1 25.2 us: route(): pl.pallas_call(functools.partial(route_kernel, nx, ny, size_x * size_y *...]
    unnamed x13 -> x2, local copies, waits for them, and re-layouts: 3.41 us -> 0.01 us
where the time goes in v2:
time: 58.5 us; the launch traced here: 58.4 us
  Pallas kernels  57.7 us (99%)
  between operations  0.67 us (1%)
    pallas_call x1, Pallas kernels, route(): pl.pallas_call(functools.partial(route_kernel, nx, ny, size_x * size_y *...  25.2 us
    pallas_call x1, Pallas kernels, finish(): pl.pallas_call(functools.partial(finish_kernel, nx, ny), out_shape=[field...  12.6 us
    pallas_call x1, Pallas kernels, share(): pl.pallas_call(functools.partial(share_kernel, nx, ny), out_shape=[f32(3,...  12.3 us
    pallas_call x1, Pallas kernels, scatter(): pl.pallas_call(functools.partial(scatter_kernel, cap), out_shape=jax.Shap...  7.49 us

profile of v2, /device:TPU:0, one launch (start us, length us, event | category | flops | bytes accessed | tf_op | source)
XLA Modules:
  0.0 58.4 jit_solution(1410153878832891753)
XLA Ops:
  0.6 25.2 %route.1 = (f32[128,128]{1,0:T(8,128)S(1)}, s32[32,128]{1,0:T(8,128)S(1)}, f32[3,36,48,128]{3,2,1,0:T(8,128)S(1)}, f32[3,32,40,128]{3,2,1,0:T(8,128)S(1)}, f32[3...) custom-call(f32[1024,128]{1,0:T(8,128)} %data_in.1, s32[8,128]{1,0:T(8,128)} %bitcast.6, s32[8,128]{1,0:T(8,128)} %bitcast.7, ...), custom_call_target="tpu_custom_call" | custom-call | tf_op jit(solution)/shard_map/route/pallas_call | solution.py:408
  25.9 0.0 copy-start
  25.9 7.5 %scatter.1 = f32[15360,128]{1,0:T(8,128)S(1)} custom-call(s32[32,128]{1,0:T(8,128)S(1)} %get-tuple-element.14.code_ref, f32[128,128]{1,0:T(8,128)S(1)} %get-tuple-element.15.got_ref), custom_call_target="tpu_custom_call" | custom-call | tf_op jit(solution)/shard_map/scatter/pallas_call | solution.py:505
  33.4 0.0 copy-done
  33.4 12.3 %share.1 = (f32[3,36,48,128]{3,2,1,0:T(8,128)S(1)}, f32[3,36,48,128]{3,2,1,0:T(8,128)S(1)}, f32[32,40,128]{2,1,0:T(8,128)S(1)}) custom-call(f32[3,32,40,128]{3,2,1,0:T(8,128)S(1)} %get-tuple-element.12.base, f32[36,48,128]{2,1,0:T(8,128)S(1)} %get-tuple-element.13.gain, f32[3,32,160,128]{3,2,1,0:T(8,128)S(1)} %bitcast.4, bf16[3,3,32,40,128]{4,3,2,1,0:T(8,128)(2,1)S(1)} %copy-done), custom_call_target="tpu_custom_call" | custom-call | tf_op jit(solution)/shard_map/share/pallas_call | solution.py:589
  45.7 12.6 %finish.1 = (f32[3,32,40,128]{3,2,1,0:T(8,128)}, f32[3,32,40,128]{3,2,1,0:T(8,128)}, f32[32,40,128]{2,1,0:T(8,128)}) custom-call(f32[3,36,48,128]{3,2,1,0:T(8,128)S(1)} %get-tuple-element.16.e1, f32[3,36,48,128]{3,2,1,0:T(8,128)S(1)} %get-tuple-element.17.h1, f32[36,48,128]{2,1,0:T(8,128)S(1)} %get-tuple-element.18.decay, ...), custom_call_target="tpu_custom_call" | custom-call | tf_op jit(solution)/shard_map/finish/pallas_call | solution.py:686
Async XLA Ops:
  25.9 7.5 %copy-start = (bf16[3,3,32,40,128]{4,3,2,1,0:T(8,128)(2,1)S(1)}, bf16[3,3,32,40,128]{4,3,2,1,0:T(8,128)(2,1)}, u32[]{:S(2)}) copy-start(bf16[3,3,32,40,128]{4,3,2,1,0:T(8,128)(2,1)} %fwd.3) | copy-start | bytes 8847364

commit v3 on v2

--- a/solution.py
+++ b/solution.py
@@ -14,6 +14,7 @@
 SPAN = LANES // FIELDS
 MESH = pl.DeviceIdType.MESH
 GROUP = 12
+PARTS = 4
 MIB = 1 << 20
 
 time_step = 0.55
@@ -74,6 +75,18 @@
         for term in split3(spread):
             packed = packed + mm(hot, term, ((1,), (1,)))
     return packed
+
+
+def sweep(start, count, body, width):
+    def several(n, _):
+        for k in range(width):
+            body(start + n * width + k)
+        return 0
+
+    turns = count // width
+    lax.fori_loop(0, turns, several, 0)
+    for p in range(turns * width, count):
+        body(start + p)
 
 
 class Place:
@@ -251,7 +264,7 @@
     for copy in loads:
         copy.wait()
 
-    def stage(x, _):
+    def stage(x):
         p = x + 2
         n = 0
         for array in (e, h):
@@ -264,9 +277,8 @@
             dn_put[n, x] = array[p, 0:1, :]
             up_put[n, x] = array[p, size_y - 1 : size_y, :]
             n += 1
-        return 0
-
-    lax.fori_loop(0, size_x, stage, 0)
+
+    sweep(0, size_x, stage, 4)
     pl.semaphore_wait(barrier, nx + ny + 2)
     halos = start_copies(
         row_copies(dn_put, up_put, up_got, lo_got, size_x, place)
@@ -324,7 +336,7 @@
             for array in (e, h):
                 array[c, p, :size_y] = array[c, p, :size_y] * keep
 
-    def unstage(p, _):
+    def unstage(p):
         keep = place.plane(p, size_x)
         above, below = keep * place.keep_hi_y, keep * place.keep_lo_y
         n = 0
@@ -336,9 +348,8 @@
                     axis=0,
                 )
                 n += 2
-        return 0
-
-    lax.fori_loop(0, size_x + 4, unstage, 0)
+
+    sweep(0, size_x + 4, unstage, 4)
     row = lax.broadcasted_iota(jnp.int32, (rows, depth), 0)
     inside = jnp.where(
         row < size_y,
@@ -347,7 +358,7 @@
     )
     ones = jnp.ones((6, depth), jnp.float32)
 
-    def coefficients(p, _):
+    def coefficients(p):
         decay[p, size_y:] = jnp.concatenate([up_got[12, p], ones, lo_got[12, p]], axis=0)
         gain[p, size_y:] = jnp.concatenate([up_got[13, p], ones, lo_got[13, p]], axis=0)
         half_loss = decay[p] * (0.5 * time_step)
@@ -356,26 +367,23 @@
         keep = inside * place.plane(p, size_x)
         decay[p] = (eps - half_loss) * inverse * keep
         gain[p] = time_step * inverse * keep
-        return 0
-
-    lax.fori_loop(1, size_x + 3, coefficients, 0)
+
+    sweep(1, size_x + 2, coefficients, 2)
     moves = shifts(rows, depth)
     factor = h_factor(place, size_y, rows, depth)
 
-    def h_step(p, _):
+    def h_step(p):
         h_plane(e, h, h, p, factor * place.plane(p, size_x), moves)
-        return 0
-
-    lax.fori_loop(0, size_x + 3, h_step, 0)
-
-    def e_step(x, _):
+
+    sweep(0, size_x + 3, h_step, 7)
+
+    def e_step(x):
         p = x + 2
         for c, curl in enumerate(curl_h(h, p, moves)):
             new = decay[p] * e[c, p] + gain[p] * curl
             base[c, x] = new[:size_y]
-        return 0
-
-    lax.fori_loop(0, size_x, e_step, 0)
+
+    sweep(0, size_x, e_step, 8)
 
     for copy in later:
         copy.wait()
@@ -526,7 +534,7 @@
     for other in others:
         pl.semaphore_signal(barrier, inc=1, device_id=other, device_id_type=MESH)
 
-    def own(x, _):
+    def own(x):
         p = x + 2
         rise = gain[p, :size_y]
         for c in range(3):
@@ -539,9 +547,8 @@
                 up_put[2 * c + r, x] = new[size_y - 2 + r : size_y - 1 + r]
             dn_put[6 + c, x] = source[:1]
             up_put[6 + c, x] = source[size_y - 1 :]
-        return 0
-
-    lax.fori_loop(0, size_x, own, 0)
+
+    sweep(0, size_x, own, 4)
     pl.semaphore_wait(barrier, len(others))
     copies = start_copies(
         row_copies(dn_put, up_put, up_got, lo_got, size_x, place)
@@ -551,14 +558,13 @@
         recv,
     )
 
-    def product(x, _):
+    def product(x):
         total = fwd[0, 0, x].astype(jnp.float32) * e[0, x + 2, :size_y]
         for c in (1, 2):
             total = total + fwd[0, c, x].astype(jnp.float32) * e[c, x + 2, :size_y]
         grad[x] = total
-        return 0
-
-    lax.fori_loop(0, size_x, product, 0)
+
+    sweep(0, size_x, product, 4)
     for copy in copies:
         copy.wait()
     for p in (0, 1, size_x + 2, size_x + 3):
@@ -566,7 +572,7 @@
         for c in range(3):
             e[c, p, :size_y] = e[c, p, :size_y] * keep
 
-    def unstage(p, _):
+    def unstage(p):
         keep = place.plane(p, size_x)
         above, below = keep * place.keep_hi_y, keep * place.keep_lo_y
         gap = jnp.zeros((4, depth), jnp.float32)
@@ -577,9 +583,8 @@
                 axis=0,
             )
             src1[c, p, size_y:] = jnp.concatenate([up_got[6 + c, p], gap, gap[:2], lo_got[6 + c, p]], axis=0)
-        return 0
-
-    lax.fori_loop(0, size_x + 4, unstage, 0)
+
+    sweep(0, size_x + 4, unstage, 4)
 
 
 def share(nx, ny, base, gain, src, fwd):
@@ -615,11 +620,10 @@
     moves = shifts(rows, depth)
     factor = h_factor(place, size_y, rows, depth)
 
-    def h_second(p, _):
+    def h_second(p):
         h_plane(e1, h1, h, p, factor * place.plane(p, size_x), moves)
-        return 0
-
-    lax.fori_loop(0, size_x + 3, h_second, 0)
+
+    sweep(0, size_x + 3, h_second, 7)
 
     def e_second(p, inner):
         fade, rise = decay[p], gain[p]
@@ -635,23 +639,21 @@
 
     e_second(1, False)
 
-    def e_inner(x, _):
-        e_second(x + 2, True)
-        return 0
-
-    lax.fori_loop(0, size_x, e_inner, 0)
+    def e_inner(p):
+        e_second(p, True)
+
+    sweep(2, size_x, e_inner, 8)
     e_second(size_x + 2, False)
 
-    def h_third(p, _):
+    def h_third(p):
         h_plane(e, h, h, p, factor * place.plane(p, size_x), moves)
-        return 0
-
-    lax.fori_loop(1, size_x + 2, h_third, 0)
+
+    sweep(1, size_x + 1, h_third, 11)
     inside = pl.ds(0, size_y)
-    outs = [pltpu.make_async_copy(h.at[:, pl.ds(2, size_x), inside], h_out, sem.at[0])]
-    outs[0].start()
-
-    def e_third(x, _):
+    h_copy = pltpu.make_async_copy(h.at[:, pl.ds(2, size_x), inside], h_out, sem.at[0])
+    h_copy.start()
+
+    def e_third(x):
         p = x + 2
         fade, rise = decay[p, :size_y], gain[p, :size_y]
         total = grad[x]
@@ -661,23 +663,28 @@
             e[c, p, :size_y] = new
             total = total + fwd[2, c, x].astype(jnp.float32) * new
         grad[x] = total
+
+    each = size_x // PARTS
+
+    def results(k):
+        here = pl.ds(k * each, each)
+        return (
+            pltpu.make_async_copy(e.at[:, pl.ds(2 + k * each, each), inside], e_out.at[:, here], sem.at[1 + 2 * k]),
+            pltpu.make_async_copy(grad.at[here], grad_out.at[here], sem.at[2 + 2 * k]),
+        )
+
+    def part(k, _):
+        for x in range(each):
+            e_third(k * each + x)
+        for copy in results(k):
+            copy.start()
         return 0
 
-    parts = 4
-    each = size_x // parts
-    for k in range(parts):
-        lax.fori_loop(k * each, (k + 1) * each, e_third, 0)
-        here = pl.ds(k * each, each)
-        outs.append(
-            pltpu.make_async_copy(
-                e.at[:, pl.ds(2 + k * each, each), inside], e_out.at[:, here], sem.at[1 + 2 * k]
-            )
-        )
-        outs.append(pltpu.make_async_copy(grad.at[here], grad_out.at[here], sem.at[2 + 2 * k]))
-        outs[-2].start()
-        outs[-1].start()
-    for copy in outs:
-        copy.wait()
+    lax.fori_loop(0, PARTS, part, 0)
+    h_copy.wait()
+    for k in range(PARTS):
+        for copy in results(k):
+            copy.wait()
 
 
 def finish(nx, ny, e1, h1, decay, gain, src1, src, fwd, grad1):
@@ -692,7 +699,7 @@
             pltpu.VMEM(e1.shape, jnp.float32),
             pltpu.VMEM(h1.shape, jnp.float32),
             pltpu.VMEM(grad1.shape, jnp.float32),
-            pltpu.SemaphoreType.DMA((9,)),
+            pltpu.SemaphoreType.DMA((1 + 2 * PARTS,)),
         ],
         compiler_params=pltpu.CompilerParams(vmem_limit_bytes=10 * MIB),
         name="finish",

time: 58.5 us -> 45.9 us (0.78)
  Pallas kernels: 57.7 us -> 45.1 us
    pallas_call x1, Pallas kernels: 12.6 us -> 4.89 us  [finish(): pl.pallas_call(functools.partial(finish_kernel, nx, ny), out_shape=[field...]
    pallas_call x1, Pallas kernels: 25.2 us -> 20.6 us  [route(): pl.pallas_call(functools.partial(route_kernel, nx, ny, size_x * size_y *...]
where the time goes in v3:
time: 45.9 us; the launch traced here: 45.8 us
  Pallas kernels  45.1 us (98%)
  between operations  0.67 us (1%)
    pallas_call x1, Pallas kernels, route(): pl.pallas_call(functools.partial(route_kernel, nx, ny, size_x * size_y *...  20.6 us
    pallas_call x1, Pallas kernels, share(): pl.pallas_call(functools.partial(share_kernel, nx, ny), out_shape=[f32(3,...  12.2 us
    pallas_call x1, Pallas kernels, scatter(): pl.pallas_call(functools.partial(scatter_kernel, cap), out_shape=jax.Shap...  7.42 us
    pallas_call x1, Pallas kernels, finish(): pl.pallas_call(functools.partial(finish_kernel, nx, ny), out_shape=[field...  4.89 us

profile of v3, /device:TPU:0, one launch (start us, length us, event | category | flops | bytes accessed | tf_op | source)
XLA Modules:
  0.0 45.8 jit_solution(15019803734744845343)
XLA Ops:
  0.6 20.6 %route.1 = (f32[128,128]{1,0:T(8,128)S(1)}, s32[32,128]{1,0:T(8,128)S(1)}, f32[3,36,48,128]{3,2,1,0:T(8,128)S(1)}, f32[3,32,40,128]{3,2,1,0:T(8,128)S(1)}, f32[3...) custom-call(f32[1024,128]{1,0:T(8,128)} %data_in.1, s32[8,128]{1,0:T(8,128)} %bitcast.6, s32[8,128]{1,0:T(8,128)} %bitcast.7, ...), custom_call_target="tpu_custom_call" | custom-call | tf_op jit(solution)/shard_map/route/pallas_call | solution.py:416
  21.3 0.0 copy-start
  21.3 7.4 %scatter.1 = f32[15360,128]{1,0:T(8,128)S(1)} custom-call(s32[32,128]{1,0:T(8,128)S(1)} %get-tuple-element.14.code_ref, f32[128,128]{1,0:T(8,128)S(1)} %get-tuple-element.15.got_ref), custom_call_target="tpu_custom_call" | custom-call | tf_op jit(solution)/shard_map/scatter/pallas_call | solution.py:513
  28.7 0.0 copy-done
  28.7 12.2 %share.1 = (f32[3,36,48,128]{3,2,1,0:T(8,128)S(1)}, f32[3,36,48,128]{3,2,1,0:T(8,128)S(1)}, f32[32,40,128]{2,1,0:T(8,128)S(1)}) custom-call(f32[3,32,40,128]{3,2,1,0:T(8,128)S(1)} %get-tuple-element.12.base, f32[36,48,128]{2,1,0:T(8,128)S(1)} %get-tuple-element.13.gain, f32[3,32,160,128]{3,2,1,0:T(8,128)S(1)} %bitcast.4, bf16[3,3,32,40,128]{4,3,2,1,0:T(8,128)(2,1)S(1)} %copy-done), custom_call_target="tpu_custom_call" | custom-call | tf_op jit(solution)/shard_map/share/pallas_call | solution.py:594
  40.9 4.9 %finish.1 = (f32[3,32,40,128]{3,2,1,0:T(8,128)}, f32[3,32,40,128]{3,2,1,0:T(8,128)}, f32[32,40,128]{2,1,0:T(8,128)}) custom-call(f32[3,36,48,128]{3,2,1,0:T(8,128)S(1)} %get-tuple-element.16.e1, f32[3,36,48,128]{3,2,1,0:T(8,128)S(1)} %get-tuple-element.17.h1, f32[36,48,128]{2,1,0:T(8,128)S(1)} %get-tuple-element.18.decay, ...), custom_call_target="tpu_custom_call" | custom-call | tf_op jit(solution)/shard_map/finish/pallas_call | solution.py:693
Async XLA Ops:
  21.3 7.4 %copy-start = (bf16[3,3,32,40,128]{4,3,2,1,0:T(8,128)(2,1)S(1)}, bf16[3,3,32,40,128]{4,3,2,1,0:T(8,128)(2,1)}, u32[]{:S(2)}) copy-start(bf16[3,3,32,40,128]{4,3,2,1,0:T(8,128)(2,1)} %fwd.3) | copy-start | bytes 8847364

commit v4 on v3

--- a/solution.py
+++ b/solution.py
@@ -13,7 +13,7 @@
 FIELDS = 4
 SPAN = LANES // FIELDS
 MESH = pl.DeviceIdType.MESH
-GROUP = 12
+GROUP = 8
 PARTS = 4
 MIB = 1 << 20
 
@@ -33,47 +33,56 @@
 
 
 def time_kernel():
-    rows = 8
-    sample = lax.broadcasted_iota(jnp.int32, (rows, SAMPLES), 1).astype(jnp.float32)
-    step = lax.broadcasted_iota(jnp.int32, (rows, SAMPLES), 0).astype(jnp.float32)
-    centre = (step + 0.5) * (SAMPLES / STEPS)
+    shape = (SAMPLES, LANES)
+    sample = lax.broadcasted_iota(jnp.int32, shape, 0).astype(jnp.float32)
+    field = lax.broadcasted_iota(jnp.int32, shape, 1) // SPAN
+    centre = (field.astype(jnp.float32) + 0.5) * (SAMPLES / STEPS)
     spread = SAMPLES / (4.0 * STEPS)
     kernel = jnp.exp(-jnp.square((sample - centre) / spread))
-    kernel = jnp.where(step < STEPS - 0.5, kernel, 0.0)
-    norm = jnp.sum(kernel * kernel, axis=1, keepdims=True)
-    return kernel / jnp.sqrt(jnp.where(norm > 0.0, norm, 1.0))
+    norm = jnp.sum(kernel * kernel, axis=0, keepdims=True)
+    return jnp.where(field < STEPS, kernel / jnp.sqrt(norm), 0.0)
 
 
 def pack(devices, cells, data_ref, tile_ref, cell_ref, comp_ref):
     blocks, width = tile_ref.shape
     kernel = time_kernel()
-    before = (
-        lax.broadcasted_iota(jnp.int32, (width, width), 0)
-        < lax.broadcasted_iota(jnp.int32, (width, width), 1)
-    ).astype(jnp.bfloat16)
+    at, to = (lax.broadcasted_iota(jnp.int32, (width, width), n) for n in (0, 1))
+    before = (at < to).astype(jnp.bfloat16)
     every = jnp.ones((width, width), jnp.bfloat16)
+    diagonal = at == to
     destination = lax.broadcasted_iota(jnp.int32, (devices, width), 0)
-    slot = lax.broadcasted_iota(jnp.int32, (SPAN, width), 0).astype(jnp.float32)
+    lane = lax.broadcasted_iota(jnp.int32, (width, LANES), 1)
+    slot = jnp.bitwise_and(lane, SPAN - 1).astype(jnp.float32)
+    is_code = lane >= STEPS * SPAN
+    down = jnp.ones((width, LANES), jnp.bfloat16)
     seen = jnp.zeros((devices, width), jnp.float32)
     packed = jnp.zeros((devices, LANES), jnp.float32)
+
+    def column(row):
+        return jnp.where(diagonal, row.astype(jnp.float32), 0.0).astype(jnp.bfloat16)
+
     for b in range(blocks):
         onehot = (destination == tile_ref[b : b + 1, :]).astype(jnp.float32)
         hot = onehot.astype(jnp.bfloat16)
         rank = jnp.sum(onehot * (seen + mm(hot, before)), axis=0, keepdims=True)
         seen = seen + mm(hot, every)
         amplitude = lax.dot_general(
+            data_ref[b * width : (b + 1) * width, :],
             kernel,
-            data_ref[b * width : (b + 1) * width, :],
-            (((1,), (1,)), ((), ())),
+            (((1,), (0,)), ((), ())),
             precision=lax.Precision.HIGHEST,
             preferred_element_type=jnp.float32,
         )
-        code = (comp_ref[b : b + 1, :] * cells + cell_ref[b : b + 1, :]).astype(jnp.float32)
-        here = slot == rank
-        fields = [amplitude[t : t + 1, :] for t in range(STEPS)] + [code]
-        spread = jnp.concatenate([jnp.where(here, f, 0.0) for f in fields], axis=0)
+        code = comp_ref[b : b + 1, :] * cells + cell_ref[b : b + 1, :]
+        low = jnp.bitwise_and(code, 255)
+        middle = jnp.bitwise_and(code, 255 << 8)
+        high = code - low - middle
+        codes = mm(column(low), down) + mm(column(middle), down) + mm(column(high), down)
+        spread = jnp.where(
+            slot == mm(column(rank), down), jnp.where(is_code, codes, amplitude), 0.0
+        )
         for term in split3(spread):
-            packed = packed + mm(hot, term, ((1,), (1,)))
+            packed = packed + mm(hot, term)
     return packed
 
 
@@ -178,6 +187,33 @@
         (part(2), part(size_x + 2), (place.lo_x, place.iy)),
         (part(size_x + 2 - count), part(2 - count), (place.hi_x, place.iy)),
     ]
+
+
+FIELD_DOWN = ((0, 0, 0), (0, 1, 0), (0, 2, 0), (0, 0, 1), (0, 2, 1))
+FIELD_UP = tuple((0, c, r) for c in range(3) for r in range(2))
+ROUTE_DOWN = (*FIELD_DOWN, (1, 0, 0), (1, 1, 0), (1, 2, 0), (2, 0, 0), (3, 0, 0))
+ROUTE_UP = (*FIELD_UP, (1, 0, 0), (1, 2, 0), (1, 0, 1), (1, 1, 1), (1, 2, 1), (2, 0, 1), (3, 0, 1))
+SHARE_DOWN = (*FIELD_DOWN, (1, 0, 0), (1, 2, 0))
+SHARE_UP = (*FIELD_UP, (1, 0, 1), (1, 1, 1), (1, 2, 1))
+
+
+def halo_scratch(down, up, size_x, depth):
+    shapes = [(len(down), size_x), (len(up), size_x), (len(down), size_x + 4), (len(up), size_x + 4)]
+    return [pltpu.VMEM((*shape, 1, depth), jnp.float32) for shape in shapes]
+
+
+def halo_rows(array, c, p, down, up, up_got, lo_got, above, below, fill):
+    def one(names, got, r, keep):
+        if (array, c, r) not in names:
+            return fill
+        return got[names.index((array, c, r)), p] * keep
+
+    return jnp.concatenate(
+        [one(down, up_got, 0, above), one(down, up_got, 1, above)]
+        + [fill] * 4
+        + [one(up, lo_got, 0, below), one(up, lo_got, 1, below)],
+        axis=0,
+    )
 
 
 def start_copies(parts, send, recv):
@@ -261,36 +297,25 @@
         pl.semaphore_signal(barrier, inc=1, device_id=(ix, lax.rem(iy + k, ny)), device_id_type=MESH)
     for other in place.corners():
         pl.semaphore_signal(barrier, inc=1, device_id=other, device_id_type=MESH)
-    for copy in loads:
+    for copy in loads[:4]:
+        copy.wait()
+    first[...] = pack(nx * ny, cells, data_ref, tile_ref, cell_ref, comp_ref)
+    for copy in loads[4:]:
         copy.wait()
 
     def stage(x):
         p = x + 2
-        n = 0
-        for array in (e, h):
-            for c in range(3):
-                for r in range(2):
-                    dn_put[n, x] = array[c, p, r : r + 1, :]
-                    up_put[n, x] = array[c, p, size_y - 2 + r : size_y - 1 + r, :]
-                    n += 1
-        for array in (decay, gain):
-            dn_put[n, x] = array[p, 0:1, :]
-            up_put[n, x] = array[p, size_y - 1 : size_y, :]
-            n += 1
+        arrays = ((e.at[0], e.at[1], e.at[2]), (h.at[0], h.at[1], h.at[2]), (decay,), (gain,))
+        for n, (array, c, r) in enumerate(ROUTE_DOWN):
+            dn_put[n, x] = arrays[array][c][p, r : r + 1, :]
+        for n, (array, c, r) in enumerate(ROUTE_UP):
+            up_put[n, x] = arrays[array][c][p, size_y - 2 + r : size_y - 1 + r, :]
 
     sweep(0, size_x, stage, 4)
     pl.semaphore_wait(barrier, nx + ny + 2)
     halos = start_copies(
-        row_copies(dn_put, up_put, up_got, lo_got, size_x, place)
-        + plane_copies(e, 2, size_x, size_y, place)
-        + plane_copies(h, 2, size_x, size_y, place)
-        + plane_copies(decay, 1, size_x, size_y, place)
-        + plane_copies(gain, 1, size_x, size_y, place),
-        send,
-        recv,
-    )
-    first[...] = pack(nx * ny, cells, data_ref, tile_ref, cell_ref, comp_ref)
-
+        row_copies(dn_put, up_put, up_got, lo_got, size_x, place), send.at[0], recv.at[0]
+    )
     copies = []
     for k in range(1, nx):
         to = lax.rem(ix + k, nx)
@@ -304,6 +329,14 @@
         )
         copy.start()
         copies.append(copy)
+    halos += start_copies(
+        plane_copies(e, 2, size_x, size_y, place)
+        + plane_copies(h, 2, size_x, size_y, place)
+        + plane_copies(decay, 1, size_x, size_y, place)
+        + plane_copies(gain, 1, size_x, size_y, place),
+        send.at[1],
+        recv.at[1],
+    )
     own = pl.ds(pl.multiple_of(ix * ny, ny), ny)
     mid[own, :] = first[own, :]
     for copy in copies:
@@ -339,15 +372,12 @@
     def unstage(p):
         keep = place.plane(p, size_x)
         above, below = keep * place.keep_hi_y, keep * place.keep_lo_y
-        n = 0
-        gap = jnp.zeros((4, depth), jnp.float32)
-        for array in (e, h):
+        gap = jnp.zeros((1, depth), jnp.float32)
+        for array, field in enumerate((e, h)):
             for c in range(3):
-                array[c, p, size_y:] = jnp.concatenate(
-                    [up_got[n, p] * above, up_got[n + 1, p] * above, gap, lo_got[n, p] * below, lo_got[n + 1, p] * below],
-                    axis=0,
+                field[c, p, size_y:] = halo_rows(
+                    array, c, p, ROUTE_DOWN, ROUTE_UP, up_got, lo_got, above, below, gap
                 )
-                n += 2
 
     sweep(0, size_x + 4, unstage, 4)
     row = lax.broadcasted_iota(jnp.int32, (rows, depth), 0)
@@ -356,11 +386,11 @@
         1.0,
         jnp.where(row == size_y, place.keep_hi_y, jnp.where(row == rows - 1, place.keep_lo_y, 0.0)),
     )
-    ones = jnp.ones((6, depth), jnp.float32)
+    ones = jnp.ones((1, depth), jnp.float32)
 
     def coefficients(p):
-        decay[p, size_y:] = jnp.concatenate([up_got[12, p], ones, lo_got[12, p]], axis=0)
-        gain[p, size_y:] = jnp.concatenate([up_got[13, p], ones, lo_got[13, p]], axis=0)
+        for array, field in ((2, decay), (3, gain)):
+            field[p, size_y:] = halo_rows(array, 0, p, ROUTE_DOWN, ROUTE_UP, up_got, lo_got, 1.0, 1.0, ones)
         half_loss = decay[p] * (0.5 * time_step)
         eps = gain[p]
         inverse = 1.0 / (eps + half_loss)
@@ -412,7 +442,6 @@
     wide, tall = size_x + 4, size_y + 8
     inputs = (data, tile, cell, comp, e, h, cond, perm)
     rows = lambda: pltpu.VMEM((devices, LANES), jnp.float32)
-    count = 14
     return pl.pallas_call(
         functools.partial(route_kernel, nx, ny, size_x * size_y * depth),
         out_shape=[
@@ -432,17 +461,14 @@
             rows(),
             rows(),
             rows(),
-            pltpu.VMEM((count, size_x, 1, depth), jnp.float32),
-            pltpu.VMEM((count, size_x, 1, depth), jnp.float32),
-            pltpu.VMEM((count, wide, 1, depth), jnp.float32),
-            pltpu.VMEM((count, wide, 1, depth), jnp.float32),
+            *halo_scratch(ROUTE_DOWN, ROUTE_UP, size_x, depth),
             pltpu.SemaphoreType.DMA((8,)),
             pltpu.SemaphoreType.DMA((ny - 1,)),
             pltpu.SemaphoreType.DMA((ny - 1,)),
             pltpu.SemaphoreType.DMA((nx - 1,)),
             pltpu.SemaphoreType.DMA((nx - 1,)),
-            pltpu.SemaphoreType.DMA((14,)),
-            pltpu.SemaphoreType.DMA((14,)),
+            pltpu.SemaphoreType.DMA((2, 8)),
+            pltpu.SemaphoreType.DMA((2, 8)),
         ],
         compiler_params=pltpu.CompilerParams(
             collective_id=0, has_side_effects=True, vmem_limit_bytes=16 * MIB
@@ -451,7 +477,9 @@
     )(*(pltpu.with_memory_space_constraint(a, pltpu.HBM) for a in inputs))
 
 
-def scatter_kernel(cap, code_ref, got_ref, out_ref, quad, wide):
+def scatter_kernel(cap, code_in, got_ref, out_ref, code_ref, quad, terms, wide, sem):
+    fetch = pltpu.make_async_copy(code_in, code_ref, sem)
+    fetch.start()
     devices = got_ref.shape[0]
     got = got_ref[...]
     lane = lax.broadcasted_iota(jnp.int32, (devices, LANES), 1)
@@ -471,23 +499,22 @@
     values = quad[...]
     high = values.astype(jnp.bfloat16)
     low = (values - high.astype(jnp.float32)).astype(jnp.bfloat16)
-    terms = jnp.concatenate([high, low], axis=1)
+    terms[:, :LANES] = high
+    terms[:, LANES:] = low
     row_slot = jnp.bitwise_and(lax.broadcasted_iota(jnp.int32, (2 * LANES, 2 * LANES), 0), SPAN - 1)
     column = lax.broadcasted_iota(jnp.int32, (2 * LANES, 2 * LANES), 1) // LANES
     for i in range(0, cap, 2):
-        pick = (row_slot == column + i).astype(jnp.bfloat16)
-        both = mm(terms, pick)
+        both = mm(terms[...], (row_slot == column + i).astype(jnp.bfloat16))
         wide[i] = both[:, :LANES]
         wide[i + 1] = both[:, LANES:]
-
-    rows = out_ref.shape[0]
-    step = 128
+    step = 512
 
     def clear(n, _):
         out_ref[pl.ds(pl.multiple_of(n * step, step), step), :] = jnp.zeros((step, LANES), jnp.float32)
         return 0
 
-    lax.fori_loop(0, rows // step, clear, 0)
+    lax.fori_loop(0, out_ref.shape[0] // step, clear, 0)
+    fetch.wait()
     depth = lax.broadcasted_iota(jnp.int32, (FIELDS, LANES), 1)
 
     def place(q, _):
@@ -513,11 +540,14 @@
     return pl.pallas_call(
         functools.partial(scatter_kernel, cap),
         out_shape=jax.ShapeDtypeStruct((rows * FIELDS, LANES), jnp.float32),
-        in_specs=[pl.BlockSpec(memory_space=pltpu.SMEM), pl.BlockSpec(memory_space=pltpu.VMEM)],
+        in_specs=[pl.BlockSpec(memory_space=pltpu.VMEM)] * 2,
         out_specs=pl.BlockSpec(memory_space=pltpu.VMEM),
         scratch_shapes=[
+            pltpu.SMEM(codes.shape, jnp.int32),
             pltpu.VMEM((devices * FIELDS, LANES), jnp.float32),
+            pltpu.VMEM((devices * FIELDS, 2 * LANES), jnp.bfloat16),
             pltpu.VMEM((cap, devices * FIELDS, LANES), jnp.float32),
+            pltpu.SemaphoreType.DMA,
         ],
         compiler_params=pltpu.CompilerParams(vmem_limit_bytes=24 * MIB),
         name="scatter",
@@ -542,11 +572,12 @@
             e[c, p, :size_y] = new
             source = src[c, x, pl.ds(1, size_y, stride=FIELDS), :]
             src1[c, p, :size_y] = source
-            for r in range(2):
-                dn_put[2 * c + r, x] = new[r : r + 1]
-                up_put[2 * c + r, x] = new[size_y - 2 + r : size_y - 1 + r]
-            dn_put[6 + c, x] = source[:1]
-            up_put[6 + c, x] = source[size_y - 1 :]
+            for n, (array, comp, r) in enumerate(SHARE_DOWN):
+                if comp == c:
+                    dn_put[n, x] = (new, source)[array][r : r + 1]
+            for n, (array, comp, r) in enumerate(SHARE_UP):
+                if comp == c:
+                    up_put[n, x] = (new, source)[array][size_y - 2 + r : size_y - 1 + r]
 
     sweep(0, size_x, own, 4)
     pl.semaphore_wait(barrier, len(others))
@@ -575,14 +606,12 @@
     def unstage(p):
         keep = place.plane(p, size_x)
         above, below = keep * place.keep_hi_y, keep * place.keep_lo_y
-        gap = jnp.zeros((4, depth), jnp.float32)
-        for c in range(3):
-            n = 2 * c
-            e[c, p, size_y:] = jnp.concatenate(
-                [up_got[n, p] * above, up_got[n + 1, p] * above, gap, lo_got[n, p] * below, lo_got[n + 1, p] * below],
-                axis=0,
-            )
-            src1[c, p, size_y:] = jnp.concatenate([up_got[6 + c, p], gap, gap[:2], lo_got[6 + c, p]], axis=0)
+        gap = jnp.zeros((1, depth), jnp.float32)
+        for array, field in enumerate((e, src1)):
+            for c in range(3):
+                field[c, p, size_y:] = halo_rows(
+                    array, c, p, SHARE_DOWN, SHARE_UP, up_got, lo_got, above, below, gap
+                )
 
     sweep(0, size_x + 4, unstage, 4)
 
@@ -590,17 +619,13 @@
 def share(nx, ny, base, gain, src, fwd):
     size_x, size_y, depth = base.shape[1:]
     wide, tall = size_x + 4, size_y + 8
-    count = 9
     return pl.pallas_call(
         functools.partial(share_kernel, nx, ny),
         out_shape=[f32(3, wide, tall, depth), f32(3, wide, tall, depth), f32(size_x, size_y, depth)],
         in_specs=in_vmem(4),
         out_specs=in_vmem(3),
         scratch_shapes=[
-            pltpu.VMEM((count, size_x, 1, depth), jnp.float32),
-            pltpu.VMEM((count, size_x, 1, depth), jnp.float32),
-            pltpu.VMEM((count, wide, 1, depth), jnp.float32),
-            pltpu.VMEM((count, wide, 1, depth), jnp.float32),
+            *halo_scratch(SHARE_DOWN, SHARE_UP, size_x, depth),
             pltpu.SemaphoreType.DMA((10,)),
             pltpu.SemaphoreType.DMA((10,)),
         ],

time: 45.9 us -> 45.9 us (level)
    pallas_call x1, Pallas kernels: 20.6 us -> 21.2 us  [route(): pl.pallas_call(functools.partial(route_kernel, nx, ny, size_x * size_y *...]
    pallas_call x1, Pallas kernels: 7.42 us -> 6.91 us  [scatter(): pl.pallas_call(functools.partial(scatter_kernel, cap), out_shape=jax.Shap...]
where the time goes in v4:
time: 45.9 us; the launch traced here: 45.8 us
  Pallas kernels  45.1 us (98%)
  between operations  0.67 us (1%)
    pallas_call x1, Pallas kernels, route(): pl.pallas_call(functools.partial(route_kernel, nx, ny, size_x * size_y *...  21.2 us
    pallas_call x1, Pallas kernels, share(): pl.pallas_call(functools.partial(share_kernel, nx, ny), out_shape=[f32(3,...  12.2 us
    pallas_call x1, Pallas kernels, scatter(): pl.pallas_call(functools.partial(scatter_kernel, cap), out_shape=jax.Shap...  6.91 us
    pallas_call x1, Pallas kernels, finish(): pl.pallas_call(functools.partial(finish_kernel, nx, ny), out_shape=[field...  4.89 us

profile of v4, /device:TPU:0, one launch (start us, length us, event | category | flops | bytes accessed | tf_op | source)
XLA Modules:
  0.0 45.8 jit_solution(17422534819068317592)
XLA Ops:
  0.6 21.2 %route.1 = (f32[128,128]{1,0:T(8,128)S(1)}, s32[32,128]{1,0:T(8,128)S(1)}, f32[3,36,48,128]{3,2,1,0:T(8,128)S(1)}, f32[3,32,40,128]{3,2,1,0:T(8,128)S(1)}, f32[3...) custom-call(f32[1024,128]{1,0:T(8,128)} %data_in.1, s32[8,128]{1,0:T(8,128)} %bitcast.6, s32[8,128]{1,0:T(8,128)} %bitcast.7, ...), custom_call_target="tpu_custom_call" | custom-call | tf_op jit(solution)/shard_map/route/pallas_call | solution.py:445
  21.8 0.0 copy-start
  21.8 6.9 %scatter.1 = f32[15360,128]{1,0:T(8,128)S(1)} custom-call(s32[32,128]{1,0:T(8,128)S(1)} %get-tuple-element.14.code_in, f32[128,128]{1,0:T(8,128)S(1)} %get-tuple-element.15.got_ref), custom_call_target="tpu_custom_call" | custom-call | tf_op jit(solution)/shard_map/scatter/pallas_call | solution.py:540
  28.7 0.0 copy-done
  28.8 12.2 %share.1 = (f32[3,36,48,128]{3,2,1,0:T(8,128)S(1)}, f32[3,36,48,128]{3,2,1,0:T(8,128)S(1)}, f32[32,40,128]{2,1,0:T(8,128)S(1)}) custom-call(f32[3,32,40,128]{3,2,1,0:T(8,128)S(1)} %get-tuple-element.12.base, f32[36,48,128]{2,1,0:T(8,128)S(1)} %get-tuple-element.13.gain, f32[3,32,160,128]{3,2,1,0:T(8,128)S(1)} %bitcast.4, bf16[3,3,32,40,128]{4,3,2,1,0:T(8,128)(2,1)S(1)} %copy-done), custom_call_target="tpu_custom_call" | custom-call | tf_op jit(solution)/shard_map/share/pallas_call | solution.py:622
  40.9 4.9 %finish.1 = (f32[3,32,40,128]{3,2,1,0:T(8,128)}, f32[3,32,40,128]{3,2,1,0:T(8,128)}, f32[32,40,128]{2,1,0:T(8,128)}) custom-call(f32[3,36,48,128]{3,2,1,0:T(8,128)S(1)} %get-tuple-element.16.e1, f32[3,36,48,128]{3,2,1,0:T(8,128)S(1)} %get-tuple-element.17.h1, f32[36,48,128]{2,1,0:T(8,128)S(1)} %get-tuple-element.18.decay, ...), custom_call_target="tpu_custom_call" | custom-call | tf_op jit(solution)/shard_map/finish/pallas_call | solution.py:718
Async XLA Ops:
  21.8 6.9 %copy-start = (bf16[3,3,32,40,128]{4,3,2,1,0:T(8,128)(2,1)S(1)}, bf16[3,3,32,40,128]{4,3,2,1,0:T(8,128)(2,1)}, u32[]{:S(2)}) copy-start(bf16[3,3,32,40,128]{4,3,2,1,0:T(8,128)(2,1)} %fwd.3) | copy-start | bytes 8847364

commit v5 on v4

--- a/solution.py
+++ b/solution.py
@@ -102,22 +102,37 @@
     def __init__(self, nx, ny):
         self.nx, self.ny = nx, ny
         self.ix, self.iy = lax.axis_index("gx"), lax.axis_index("gy")
-        self.lo_x, self.hi_x = lax.rem(self.ix + nx - 1, nx), lax.rem(self.ix + 1, nx)
-        self.lo_y, self.hi_y = lax.rem(self.iy + ny - 1, ny), lax.rem(self.iy + 1, ny)
-        one, zero = jnp.float32(1.0), jnp.float32(0.0)
-        self.keep_lo_x = jnp.where(self.ix == 0, zero, one)
-        self.keep_hi_x = jnp.where(self.ix == nx - 1, zero, one)
-        self.keep_lo_y = jnp.where(self.iy == 0, zero, one)
-        self.keep_hi_y = jnp.where(self.iy == ny - 1, zero, one)
-
-    def corners(self):
-        return [(x, y) for x in (self.lo_x, self.hi_x) for y in (self.lo_y, self.hi_y)]
-
-    def sides(self):
-        return [(self.lo_x, self.iy), (self.hi_x, self.iy), (self.ix, self.lo_y), (self.ix, self.hi_y)]
+        self.inside_x = {-1: self.ix > 0, 0: None, 1: self.ix < nx - 1}
+        self.inside_y = {-1: self.iy > 0, 0: None, 1: self.iy < ny - 1}
+
+    def other(self, dx, dy):
+        return lax.rem(self.ix + dx + self.nx, self.nx), lax.rem(self.iy + dy + self.ny, self.ny)
+
+    def has(self, dx, dy):
+        x, y = self.inside_x[dx], self.inside_y[dy]
+        if x is None or y is None:
+            return y if x is None else x
+        return jnp.logical_and(x, y)
 
     def plane(self, p, size_x):
-        return jnp.where(p < 2, self.keep_lo_x, jnp.where(p >= size_x + 2, self.keep_hi_x, 1.0))
+        low, high = jnp.logical_or(p >= 2, self.ix > 0), jnp.logical_or(p < size_x + 2, self.ix < self.nx - 1)
+        return jnp.logical_and(low, high)
+
+
+AROUND = tuple((dx, dy) for dx in (-1, 0, 1) for dy in (-1, 0, 1) if (dx, dy) != (0, 0))
+
+
+def greet(place, barrier, offsets):
+    count = jnp.int32(0)
+    for dx, dy in offsets:
+        here = place.has(dx, dy)
+        count = count + here.astype(jnp.int32)
+
+        @pl.when(here)
+        def _(dx=dx, dy=dy):
+            pl.semaphore_signal(barrier, inc=1, device_id=place.other(dx, dy), device_id_type=MESH)
+
+    return count
 
 
 def shifts(rows, depth):
@@ -159,24 +174,24 @@
 
 def h_factor(place, size_y, rows, depth):
     row = lax.broadcasted_iota(jnp.int32, (rows, depth), 0)
-    beyond = jnp.where(row < size_y + 4, place.keep_hi_y, place.keep_lo_y)
-    return time_step * jnp.where(row < size_y, 1.0, beyond)
-
-
-def row_copies(dn_put, up_put, up_got, lo_got, size_x, place):
+    above, below = jnp.where(place.has(0, 1), 1.0, 0.0), jnp.where(place.has(0, -1), 1.0, 0.0)
+    return time_step * jnp.where(row < size_y, 1.0, jnp.where(row < size_y + 4, above, below))
+
+
+def row_copies(dn_put, up_put, up_got, lo_got, size_x):
     first, last, low, high = pl.ds(0, 2), pl.ds(size_x - 2, 2), pl.ds(0, 2), pl.ds(size_x + 2, 2)
     whole = pl.ds(2, size_x)
     return [
-        (dn_put, up_got.at[:, whole], (place.ix, place.lo_y)),
-        (up_put, lo_got.at[:, whole], (place.ix, place.hi_y)),
-        (dn_put.at[:, first], up_got.at[:, high], (place.lo_x, place.lo_y)),
-        (dn_put.at[:, last], up_got.at[:, low], (place.hi_x, place.lo_y)),
-        (up_put.at[:, first], lo_got.at[:, high], (place.lo_x, place.hi_y)),
-        (up_put.at[:, last], lo_got.at[:, low], (place.hi_x, place.hi_y)),
+        (dn_put, up_got.at[:, whole], 0, -1),
+        (up_put, lo_got.at[:, whole], 0, 1),
+        (dn_put.at[:, first], up_got.at[:, high], -1, -1),
+        (dn_put.at[:, last], up_got.at[:, low], 1, -1),
+        (up_put.at[:, first], lo_got.at[:, high], -1, 1),
+        (up_put.at[:, last], lo_got.at[:, low], 1, 1),
     ]
 
 
-def plane_copies(array, count, size_x, size_y, place):
+def plane_copies(array, count, size_x, size_y):
     lead = (slice(None),) * (len(array.shape) - 3)
     rows = pl.ds(0, size_y)
 
@@ -184,8 +199,8 @@
         return array.at[(*lead, pl.ds(start, count), rows)]
 
     return [
-        (part(2), part(size_x + 2), (place.lo_x, place.iy)),
-        (part(size_x + 2 - count), part(2 - count), (place.hi_x, place.iy)),
+        (part(2), part(size_x + 2), -1, 0),
+        (part(size_x + 2 - count), part(2 - count), 1, 0),
     ]
 
 
@@ -206,7 +221,7 @@
     def one(names, got, r, keep):
         if (array, c, r) not in names:
             return fill
-        return got[names.index((array, c, r)), p] * keep
+        return jnp.where(keep, got[names.index((array, c, r)), p], fill)
 
     return jnp.concatenate(
         [one(down, up_got, 0, above), one(down, up_got, 1, above)]
@@ -216,21 +231,25 @@
     )
 
 
-def start_copies(parts, send, recv):
-    copies = [
-        pltpu.make_async_remote_copy(
-            src_ref=a,
-            dst_ref=b,
-            send_sem=send.at[n],
-            recv_sem=recv.at[n],
-            device_id=device,
-            device_id_type=MESH,
-        )
-        for n, (a, b, device) in enumerate(parts)
-    ]
-    for copy in copies:
-        copy.start()
-    return copies
+class Exchange:
+    def __init__(self, place, parts, send, recv):
+        self.parts = []
+        for n, (a, b, dx, dy) in enumerate(parts):
+            copy = pltpu.make_async_remote_copy(
+                src_ref=a,
+                dst_ref=b,
+                send_sem=send.at[n],
+                recv_sem=recv.at[n],
+                device_id=place.other(dx, dy),
+                device_id_type=MESH,
+            )
+            self.parts.append((copy, place.has(dx, dy), place.has(-dx, -dy)))
+            pl.when(self.parts[-1][1])(copy.start)
+
+    def wait(self):
+        for copy, goes, comes in self.parts:
+            pl.when(comes)(copy.wait_recv)
+            pl.when(goes)(copy.wait_send)
 
 
 def route_kernel(
@@ -295,8 +314,7 @@
         pl.semaphore_signal(barrier, inc=1, device_id=(lax.rem(ix + k, nx), iy), device_id_type=MESH)
     for k in range(1, ny):
         pl.semaphore_signal(barrier, inc=1, device_id=(ix, lax.rem(iy + k, ny)), device_id_type=MESH)
-    for other in place.corners():
-        pl.semaphore_signal(barrier, inc=1, device_id=other, device_id_type=MESH)
+    corners = greet(place, barrier, [o for o in AROUND if 0 not in o])
     for copy in loads[:4]:
         copy.wait()
     first[...] = pack(nx * ny, cells, data_ref, tile_ref, cell_ref, comp_ref)
@@ -312,9 +330,9 @@
             up_put[n, x] = arrays[array][c][p, size_y - 2 + r : size_y - 1 + r, :]
 
     sweep(0, size_x, stage, 4)
-    pl.semaphore_wait(barrier, nx + ny + 2)
-    halos = start_copies(
-        row_copies(dn_put, up_put, up_got, lo_got, size_x, place), send.at[0], recv.at[0]
+    pl.semaphore_wait(barrier, corners + (nx + ny - 2))
+    by_row = Exchange(
+        place, row_copies(dn_put, up_put, up_got, lo_got, size_x), send.at[0], recv.at[0]
     )
     copies = []
     for k in range(1, nx):
@@ -329,11 +347,12 @@
         )
         copy.start()
         copies.append(copy)
-    halos += start_copies(
-        plane_copies(e, 2, size_x, size_y, place)
-        + plane_copies(h, 2, size_x, size_y, place)
-        + plane_copies(decay, 1, size_x, size_y, place)
-        + plane_copies(gain, 1, size_x, size_y, place),
+    by_plane = Exchange(
+        place,
+        plane_copies(e, 2, size_x, size_y)
+        + plane_copies(h, 2, size_x, size_y)
+        + plane_copies(decay, 1, size_x, size_y)
+        + plane_copies(gain, 1, size_x, size_y),
         send.at[1],
         recv.at[1],
     )
@@ -361,17 +380,17 @@
     for copy in copies:
         copy.wait_send()
 
-    for copy in halos:
-        copy.wait()
+    by_plane.wait()
+    by_row.wait()
     for p in (0, 1, size_x + 2, size_x + 3):
         keep = place.plane(p, size_x)
         for c in range(3):
             for array in (e, h):
-                array[c, p, :size_y] = array[c, p, :size_y] * keep
+                array[c, p, :size_y] = jnp.where(keep, array[c, p, :size_y], 0.0)
 
     def unstage(p):
         keep = place.plane(p, size_x)
-        above, below = keep * place.keep_hi_y, keep * place.keep_lo_y
+        above, below = jnp.logical_and(keep, place.has(0, 1)), jnp.logical_and(keep, place.has(0, -1))
         gap = jnp.zeros((1, depth), jnp.float32)
         for array, field in enumerate((e, h)):
             for c in range(3):
@@ -384,26 +403,30 @@
     inside = jnp.where(
         row < size_y,
         1.0,
-        jnp.where(row == size_y, place.keep_hi_y, jnp.where(row == rows - 1, place.keep_lo_y, 0.0)),
+        jnp.where(
+            row == size_y,
+            jnp.where(place.has(0, 1), 1.0, 0.0),
+            jnp.where(row == rows - 1, jnp.where(place.has(0, -1), 1.0, 0.0), 0.0),
+        ),
     )
     ones = jnp.ones((1, depth), jnp.float32)
 
     def coefficients(p):
         for array, field in ((2, decay), (3, gain)):
-            field[p, size_y:] = halo_rows(array, 0, p, ROUTE_DOWN, ROUTE_UP, up_got, lo_got, 1.0, 1.0, ones)
+            field[p, size_y:] = halo_rows(array, 0, p, ROUTE_DOWN, ROUTE_UP, up_got, lo_got, True, True, ones)
         half_loss = decay[p] * (0.5 * time_step)
         eps = gain[p]
         inverse = 1.0 / (eps + half_loss)
-        keep = inside * place.plane(p, size_x)
-        decay[p] = (eps - half_loss) * inverse * keep
-        gain[p] = time_step * inverse * keep
+        keep = inside > jnp.where(place.plane(p, size_x), 0.5, 1.5)
+        decay[p] = jnp.where(keep, (eps - half_loss) * inverse, 0.0)
+        gain[p] = jnp.where(keep, time_step * inverse, 0.0)
 
     sweep(1, size_x + 2, coefficients, 2)
     moves = shifts(rows, depth)
     factor = h_factor(place, size_y, rows, depth)
 
     def h_step(p):
-        h_plane(e, h, h, p, factor * place.plane(p, size_x), moves)
+        h_plane(e, h, h, p, factor * jnp.where(place.plane(p, size_x), 1.0, 0.0), moves)
 
     sweep(0, size_x + 3, h_step, 7)
 
@@ -560,9 +583,7 @@
     place = Place(nx, ny)
     size_x, size_y, depth = base.shape[1:]
     barrier = pltpu.get_barrier_semaphore()
-    others = place.sides() + place.corners()
-    for other in others:
-        pl.semaphore_signal(barrier, inc=1, device_id=other, device_id_type=MESH)
+    others = greet(place, barrier, AROUND)
 
     def own(x):
         p = x + 2
@@ -580,11 +601,12 @@
                     up_put[n, x] = (new, source)[array][size_y - 2 + r : size_y - 1 + r]
 
     sweep(0, size_x, own, 4)
-    pl.semaphore_wait(barrier, len(others))
-    copies = start_copies(
-        row_copies(dn_put, up_put, up_got, lo_got, size_x, place)
-        + plane_copies(e, 2, size_x, size_y, place)
-        + plane_copies(src1, 1, size_x, size_y, place),
+    pl.semaphore_wait(barrier, others)
+    halos = Exchange(
+        place,
+        row_copies(dn_put, up_put, up_got, lo_got, size_x)
+        + plane_copies(e, 2, size_x, size_y)
+        + plane_copies(src1, 1, size_x, size_y),
         send,
         recv,
     )
@@ -596,16 +618,16 @@
         grad[x] = total
 
     sweep(0, size_x, product, 4)
-    for copy in copies:
-        copy.wait()
+    halos.wait()
     for p in (0, 1, size_x + 2, size_x + 3):
         keep = place.plane(p, size_x)
         for c in range(3):
-            e[c, p, :size_y] = e[c, p, :size_y] * keep
+            e[c, p, :size_y] = jnp.where(keep, e[c, p, :size_y], 0.0)
+            src1[c, p, :size_y] = jnp.where(keep, src1[c, p, :size_y], 0.0)
 
     def unstage(p):
         keep = place.plane(p, size_x)
-        above, below = keep * place.keep_hi_y, keep * place.keep_lo_y
+        above, below = jnp.logical_and(keep, place.has(0, 1)), jnp.logical_and(keep, place.has(0, -1))
         gap = jnp.zeros((1, depth), jnp.float32)
         for array, field in enumerate((e, src1)):
             for c in range(3):
@@ -646,7 +668,7 @@
     factor = h_factor(place, size_y, rows, depth)
 
     def h_second(p):
-        h_plane(e1, h1, h, p, factor * place.plane(p, size_x), moves)
+        h_plane(e1, h1, h, p, factor * jnp.where(place.plane(p, size_x), 1.0, 0.0), moves)
 
     sweep(0, size_x + 3, h_second, 7)
 
@@ -671,7 +693,7 @@
     e_second(size_x + 2, False)
 
     def h_third(p):
-        h_plane(e, h, h, p, factor * place.plane(p, size_x), moves)
+        h_plane(e, h, h, p, factor * jnp.where(place.plane(p, size_x), 1.0, 0.0), moves)
 
     sweep(1, size_x + 1, h_third, 11)
     inside = pl.ds(0, size_y)

time: 45.9 us -> 40.4 us (0.88)
  the two profiles are of different devices: /device:TPU:0 before, /device:TPU:9 now
where the time goes in v5:
time: 40.4 us; the launch traced here: 40.3 us
  Pallas kernels  39.6 us (98%)
  between operations  0.67 us (2%)
    pallas_call x1, Pallas kernels, route(): pl.pallas_call(functools.partial(route_kernel, nx, ny, size_x * size_y *...  17.2 us
    pallas_call x1, Pallas kernels, share(): pl.pallas_call(functools.partial(share_kernel, nx, ny), out_shape=[f32(3,...  10.8 us
    pallas_call x1, Pallas kernels, scatter(): pl.pallas_call(functools.partial(scatter_kernel, cap), out_shape=jax.Shap...  6.7 us
    pallas_call x1, Pallas kernels, finish(): pl.pallas_call(functools.partial(finish_kernel, nx, ny), out_shape=[field...  4.88 us

profile of v5, /device:TPU:9, one launch (start us, length us, event | category | flops | bytes accessed | tf_op | source)
XLA Modules:
  0.0 40.3 jit_solution(12380119605394892672)
XLA Ops:
  0.6 17.2 %route.1 = (f32[128,128]{1,0:T(8,128)S(1)}, s32[32,128]{1,0:T(8,128)S(1)}, f32[3,36,48,128]{3,2,1,0:T(8,128)S(1)}, f32[3,32,40,128]{3,2,1,0:T(8,128)S(1)}, f32[3...) custom-call(f32[1024,128]{1,0:T(8,128)} %data_in.1, s32[8,128]{1,0:T(8,128)} %bitcast.6, s32[8,128]{1,0:T(8,128)} %bitcast.7, ...), custom_call_target="tpu_custom_call" | custom-call | tf_op jit(solution)/shard_map/route/pallas_call | solution.py:468
  17.8 0.0 copy-start
  17.8 6.7 %scatter.1 = f32[15360,128]{1,0:T(8,128)S(1)} custom-call(s32[32,128]{1,0:T(8,128)S(1)} %get-tuple-element.14.code_in, f32[128,128]{1,0:T(8,128)S(1)} %get-tuple-element.15.got_ref), custom_call_target="tpu_custom_call" | custom-call | tf_op jit(solution)/shard_map/scatter/pallas_call | solution.py:563
  24.5 0.0 copy-done
  24.5 10.8 %share.1 = (f32[3,36,48,128]{3,2,1,0:T(8,128)S(1)}, f32[3,36,48,128]{3,2,1,0:T(8,128)S(1)}, f32[32,40,128]{2,1,0:T(8,128)S(1)}) custom-call(f32[3,32,40,128]{3,2,1,0:T(8,128)S(1)} %get-tuple-element.12.base, f32[36,48,128]{2,1,0:T(8,128)S(1)} %get-tuple-element.13.gain, f32[3,32,160,128]{3,2,1,0:T(8,128)S(1)} %bitcast.4, bf16[3,3,32,40,128]{4,3,2,1,0:T(8,128)(2,1)S(1)} %copy-done), custom_call_target="tpu_custom_call" | custom-call | tf_op jit(solution)/shard_map/share/pallas_call | solution.py:644
  35.4 4.9 %finish.1 = (f32[3,32,40,128]{3,2,1,0:T(8,128)}, f32[3,32,40,128]{3,2,1,0:T(8,128)}, f32[32,40,128]{2,1,0:T(8,128)}) custom-call(f32[3,36,48,128]{3,2,1,0:T(8,128)S(1)} %get-tuple-element.16.e1, f32[3,36,48,128]{3,2,1,0:T(8,128)S(1)} %get-tuple-element.17.h1, f32[36,48,128]{2,1,0:T(8,128)S(1)} %get-tuple-element.18.decay, ...), custom_call_target="tpu_custom_call" | custom-call | tf_op jit(solution)/shard_map/finish/pallas_call | solution.py:740
Async XLA Ops:
  17.8 6.7 %copy-start = (bf16[3,3,32,40,128]{4,3,2,1,0:T(8,128)(2,1)S(1)}, bf16[3,3,32,40,128]{4,3,2,1,0:T(8,128)(2,1)}, u32[]{:S(2)}) copy-start(bf16[3,3,32,40,128]{4,3,2,1,0:T(8,128)(2,1)} %fwd.3) | copy-start | bytes 8847364

commit v6 on v5

--- a/solution.py
+++ b/solution.py
@@ -182,12 +182,12 @@
     first, last, low, high = pl.ds(0, 2), pl.ds(size_x - 2, 2), pl.ds(0, 2), pl.ds(size_x + 2, 2)
     whole = pl.ds(2, size_x)
     return [
-        (dn_put, up_got.at[:, whole], 0, -1),
-        (up_put, lo_got.at[:, whole], 0, 1),
         (dn_put.at[:, first], up_got.at[:, high], -1, -1),
         (dn_put.at[:, last], up_got.at[:, low], 1, -1),
         (up_put.at[:, first], lo_got.at[:, high], -1, 1),
         (up_put.at[:, last], lo_got.at[:, low], 1, 1),
+        (dn_put, up_got.at[:, whole], 0, -1),
+        (up_put, lo_got.at[:, whole], 0, 1),
     ]
 
 
@@ -252,6 +252,10 @@
             pl.when(goes)(copy.wait_send)
 
 
+def parts_of(state):
+    return state.at[pl.ds(0, 3)], state.at[pl.ds(3, 3)], state.at[6], state.at[7]
+
+
 def route_kernel(
     nx,
     ny,
@@ -266,15 +270,12 @@
     perm_in,
     got_ref,
     code_ref,
-    h,
+    state,
     base,
-    decay,
-    gain,
     data_ref,
     tile_ref,
     cell_ref,
     comp_ref,
-    e,
     first,
     mid,
     second,
@@ -293,6 +294,7 @@
 ):
     place = Place(nx, ny)
     ix, iy = place.ix, place.iy
+    e, h, decay, gain = parts_of(state)
     size_x, size_y, depth = base.shape[1:]
     rows = size_y + 8
     inner = (pl.ds(2, size_x), pl.ds(0, size_y))
@@ -348,13 +350,7 @@
         copy.start()
         copies.append(copy)
     by_plane = Exchange(
-        place,
-        plane_copies(e, 2, size_x, size_y)
-        + plane_copies(h, 2, size_x, size_y)
-        + plane_copies(decay, 1, size_x, size_y)
-        + plane_copies(gain, 1, size_x, size_y),
-        send.at[1],
-        recv.at[1],
+        place, plane_copies(state, 2, size_x, size_y), send.at[1], recv.at[1]
     )
     own = pl.ds(pl.multiple_of(ix * ny, ny), ny)
     mid[own, :] = first[own, :]
@@ -470,16 +466,13 @@
         out_shape=[
             f32(devices, LANES),
             jax.ShapeDtypeStruct((devices // FIELDS, LANES), jnp.int32),
-            f32(3, wide, tall, depth),
+            f32(8, wide, tall, depth),
             f32(3, size_x, size_y, depth),
-            f32(wide, tall, depth),
-            f32(wide, tall, depth),
         ],
         in_specs=[pl.BlockSpec(memory_space=pltpu.HBM)] * 8,
-        out_specs=in_vmem(6),
+        out_specs=in_vmem(4),
         scratch_shapes=[
             *(pltpu.VMEM(a.shape, a.dtype) for a in (data, tile, cell, comp)),
-            pltpu.VMEM((3, wide, tall, depth), jnp.float32),
             rows(),
             rows(),
             rows(),
@@ -578,9 +571,11 @@
 
 
 def share_kernel(
-    nx, ny, base, gain, src, fwd, e, src1, grad, dn_put, up_put, up_got, lo_got, send, recv
+    nx, ny, base, state, src, fwd, both, grad, dn_put, up_put, up_got, lo_got, send, recv
 ):
     place = Place(nx, ny)
+    gain = parts_of(state)[3]
+    e, src1 = both.at[pl.ds(0, 3)], both.at[pl.ds(3, 3)]
     size_x, size_y, depth = base.shape[1:]
     barrier = pltpu.get_barrier_semaphore()
     others = greet(place, barrier, AROUND)
@@ -605,8 +600,7 @@
     halos = Exchange(
         place,
         row_copies(dn_put, up_put, up_got, lo_got, size_x)
-        + plane_copies(e, 2, size_x, size_y)
-        + plane_copies(src1, 1, size_x, size_y),
+        + plane_copies(both, 2, size_x, size_y),
         send,
         recv,
     )
@@ -638,30 +632,32 @@
     sweep(0, size_x + 4, unstage, 4)
 
 
-def share(nx, ny, base, gain, src, fwd):
+def share(nx, ny, base, state, src, fwd):
     size_x, size_y, depth = base.shape[1:]
     wide, tall = size_x + 4, size_y + 8
     return pl.pallas_call(
         functools.partial(share_kernel, nx, ny),
-        out_shape=[f32(3, wide, tall, depth), f32(3, wide, tall, depth), f32(size_x, size_y, depth)],
+        out_shape=[f32(6, wide, tall, depth), f32(size_x, size_y, depth)],
         in_specs=in_vmem(4),
-        out_specs=in_vmem(3),
+        out_specs=in_vmem(2),
         scratch_shapes=[
             *halo_scratch(SHARE_DOWN, SHARE_UP, size_x, depth),
-            pltpu.SemaphoreType.DMA((10,)),
-            pltpu.SemaphoreType.DMA((10,)),
+            pltpu.SemaphoreType.DMA((8,)),
+            pltpu.SemaphoreType.DMA((8,)),
         ],
         compiler_params=pltpu.CompilerParams(
             collective_id=1, has_side_effects=True, vmem_limit_bytes=6 * MIB
         ),
         name="share",
-    )(base, gain, src, fwd)
+    )(base, state, src, fwd)
 
 
 def finish_kernel(
-    nx, ny, e1, h1, decay, gain, src1, src, fwd, grad1, e_out, h_out, grad_out, e, h, grad, sem
+    nx, ny, both, state, src, fwd, grad1, e_out, h_out, grad_out, e, h, grad, sem
 ):
     place = Place(nx, ny)
+    e1, src1 = both.at[pl.ds(0, 3)], both.at[pl.ds(3, 3)]
+    _, h1, decay, gain = parts_of(state)
     size_x, size_y, depth = grad1.shape
     rows = size_y + 8
     moves = shifts(rows, depth)
@@ -734,23 +730,23 @@
             copy.wait()
 
 
-def finish(nx, ny, e1, h1, decay, gain, src1, src, fwd, grad1):
+def finish(nx, ny, both, state, src, fwd, grad1):
     size_x, size_y, depth = grad1.shape
     field = f32(3, size_x, size_y, depth)
     return pl.pallas_call(
         functools.partial(finish_kernel, nx, ny),
         out_shape=[field, field, f32(size_x, size_y, depth)],
-        in_specs=in_vmem(8),
+        in_specs=in_vmem(5),
         out_specs=[pl.BlockSpec(memory_space=pltpu.HBM)] * 3,
         scratch_shapes=[
-            pltpu.VMEM(e1.shape, jnp.float32),
-            pltpu.VMEM(h1.shape, jnp.float32),
+            pltpu.VMEM((3, *both.shape[1:]), jnp.float32),
+            pltpu.VMEM((3, *both.shape[1:]), jnp.float32),
             pltpu.VMEM(grad1.shape, jnp.float32),
             pltpu.SemaphoreType.DMA((1 + 2 * PARTS,)),
         ],
         compiler_params=pltpu.CompilerParams(vmem_limit_bytes=10 * MIB),
         name="finish",
-    )(e1, h1, decay, gain, src1, src, fwd, grad1)
+    )(both, state, src, fwd, grad1)
 
 
 def per_device(
@@ -769,7 +765,7 @@
     receivers = receiver_data.shape[0]
     cap = 3 * receivers // (nx * ny)
     by_lane = lambda a: a.reshape(receivers // LANES, LANES)
-    got, codes, h1, base, decay, gain = route(
+    got, codes, state, base = route(
         nx,
         ny,
         receiver_data,
@@ -783,8 +779,8 @@
     )
     placed = scatter(cap, 3 * size_x * size_y, codes, got)
     placed = placed.reshape(3, size_x, size_y * FIELDS, depth)
-    e1, src1, grad1 = share(nx, ny, base, gain, placed, forward_e)
-    return tuple(finish(nx, ny, e1, h1, decay, gain, src1, placed, forward_e, grad1))
+    both, grad1 = share(nx, ny, base, state, placed, forward_e)
+    return tuple(finish(nx, ny, both, state, placed, forward_e, grad1))
 
 
 def solution(mesh):

time: 40.4 us -> 39.2 us (0.970)
  Pallas kernels: 39.6 us -> 38.4 us
    pallas_call x1, Pallas kernels: 10.8 us -> 10.1 us  [share(): pl.pallas_call(functools.partial(share_kernel, nx, ny), out_shape=[f32(6,...]
    pallas_call x1, Pallas kernels: 17.2 us -> 16.5 us  [route(): pl.pallas_call(functools.partial(route_kernel, nx, ny, size_x * size_y *...]
where the time goes in v6:
time: 39.2 us; the launch traced here: 39 us
  Pallas kernels  38.4 us (98%)
  between operations  0.67 us (2%)
    pallas_call x1, Pallas kernels, route(): pl.pallas_call(functools.partial(route_kernel, nx, ny, size_x * size_y *...  16.5 us
    pallas_call x1, Pallas kernels, share(): pl.pallas_call(functools.partial(share_kernel, nx, ny), out_shape=[f32(6,...  10.1 us
    pallas_call x1, Pallas kernels, scatter(): pl.pallas_call(functools.partial(scatter_kernel, cap), out_shape=jax.Shap...  6.86 us
    pallas_call x1, Pallas kernels, finish(): pl.pallas_call(functools.partial(finish_kernel, nx, ny), out_shape=[field...  4.88 us

profile of v6, /device:TPU:9, one launch (start us, length us, event | category | flops | bytes accessed | tf_op | source)
XLA Modules:
  0.0 39.0 jit_solution(17645423496499364661)
XLA Ops:
  0.6 16.5 %route.1 = (f32[128,128]{1,0:T(8,128)S(1)}, s32[32,128]{1,0:T(8,128)S(1)}, f32[8,36,48,128]{3,2,1,0:T(8,128)S(1)}, f32[3,32,40,128]{3,2,1,0:T(8,128)S(1)}) custom-call(f32[1024,128]{1,0:T(8,128)} %data_in.1, s32[8,128]{1,0:T(8,128)} %bitcast.6, s32[8,128]{1,0:T(8,128)} %bitcast.7, s32[8,128]{1,0:T(8,128)} %bitcast.8, f32[3,32,40,128]{3,2,1,0:T(8,128)} %e_in.1, ...), custom_call_target="tpu_custom_call" | custom-call | tf_op jit(solution)/shard_map/route/pallas_call | solution.py:464
  17.2 0.0 copy-start
  17.2 6.9 %scatter.1 = f32[15360,128]{1,0:T(8,128)S(1)} custom-call(s32[32,128]{1,0:T(8,128)S(1)} %get-tuple-element.11.code_in, f32[128,128]{1,0:T(8,128)S(1)} %get-tuple-element.12.got_ref), custom_call_target="tpu_custom_call" | custom-call | tf_op jit(solution)/shard_map/scatter/pallas_call | solution.py:556
  24.1 0.0 copy-done
  24.1 10.1 %share.1 = (f32[6,36,48,128]{3,2,1,0:T(8,128)S(1)}, f32[32,40,128]{2,1,0:T(8,128)S(1)}) custom-call(f32[3,32,40,128]{3,2,1,0:T(8,128)S(1)} %get-tuple-element.9.base, f32[8,36,48,128]{3,2,1,0:T(8,128)S(1)} %get-tuple-element.10.state, f32[3,32,160,128]{3,2,1,0:T(8,128)S(1)} %bitcast.4, bf16[3,3,32,40,128]{4,3,2,1,0:T(8,128)(2,1)S(1)} %copy-done), custom_call_target="tpu_custom_call" | custom-call | tf_op jit(solution)/shard_map/share/pallas_call | solution.py:638
  34.2 4.9 %finish.1 = (f32[3,32,40,128]{3,2,1,0:T(8,128)}, f32[3,32,40,128]{3,2,1,0:T(8,128)}, f32[32,40,128]{2,1,0:T(8,128)}) custom-call(f32[6,36,48,128]{3,2,1,0:T(8,128)S(1)} %get-tuple-element.13.both, f32[8,36,48,128]{3,2,1,0:T(8,128)S(1)} %get-tuple-element.10.state, f32[3,32,160,128]{3,2,1,0:T(8,128)S(1)} %bitcast.5, bf16[3,3,32,40,128]{4,3,2,1,0:T(8,128)(2,1)S(1)} %copy-done, ...), custom_call_target="tpu_custom_call" | custom-call | tf_op jit(solution)/shard_map/finish/pallas_call | solution.py:736
Async XLA Ops:
  17.2 6.9 %copy-start = (bf16[3,3,32,40,128]{4,3,2,1,0:T(8,128)(2,1)S(1)}, bf16[3,3,32,40,128]{4,3,2,1,0:T(8,128)(2,1)}, u32[]{:S(2)}) copy-start(bf16[3,3,32,40,128]{4,3,2,1,0:T(8,128)(2,1)} %fwd.3) | copy-start | bytes 8847364

commit v7 on v6

--- a/solution.py
+++ b/solution.py
@@ -271,7 +271,6 @@
     got_ref,
     code_ref,
     state,
-    base,
     data_ref,
     tile_ref,
     cell_ref,
@@ -295,7 +294,7 @@
     place = Place(nx, ny)
     ix, iy = place.ix, place.iy
     e, h, decay, gain = parts_of(state)
-    size_x, size_y, depth = base.shape[1:]
+    size_x, size_y, depth = cond_in.shape
     rows = size_y + 8
     inner = (pl.ds(2, size_x), pl.ds(0, size_y))
     pairs = (
@@ -426,14 +425,6 @@
 
     sweep(0, size_x + 3, h_step, 7)
 
-    def e_step(x):
-        p = x + 2
-        for c, curl in enumerate(curl_h(h, p, moves)):
-            new = decay[p] * e[c, p] + gain[p] * curl
-            base[c, x] = new[:size_y]
-
-    sweep(0, size_x, e_step, 8)
-
     for copy in later:
         copy.wait()
     got_ref[...] = last[...]
@@ -467,10 +458,9 @@
             f32(devices, LANES),
             jax.ShapeDtypeStruct((devices // FIELDS, LANES), jnp.int32),
             f32(8, wide, tall, depth),
-            f32(3, size_x, size_y, depth),
         ],
         in_specs=[pl.BlockSpec(memory_space=pltpu.HBM)] * 8,
-        out_specs=in_vmem(4),
+        out_specs=in_vmem(3),
         scratch_shapes=[
             *(pltpu.VMEM(a.shape, a.dtype) for a in (data, tile, cell, comp)),
             rows(),
@@ -571,20 +561,22 @@
 
 
 def share_kernel(
-    nx, ny, base, state, src, fwd, both, grad, dn_put, up_put, up_got, lo_got, send, recv
+    nx, ny, state, src, fwd, both, grad, dn_put, up_put, up_got, lo_got, send, recv
 ):
     place = Place(nx, ny)
-    gain = parts_of(state)[3]
+    e0, h1, decay, gain = parts_of(state)
     e, src1 = both.at[pl.ds(0, 3)], both.at[pl.ds(3, 3)]
-    size_x, size_y, depth = base.shape[1:]
+    size_x, size_y, depth = grad.shape
+    moves = shifts(size_y + 8, depth)
     barrier = pltpu.get_barrier_semaphore()
     others = greet(place, barrier, AROUND)
 
     def own(x):
         p = x + 2
-        rise = gain[p, :size_y]
-        for c in range(3):
-            new = base[c, x] - rise * src[c, x, pl.ds(0, size_y, stride=FIELDS), :]
+        fade, rise = decay[p, :size_y], gain[p, :size_y]
+        for c, curl in enumerate(curl_h(h1, p, moves)):
+            source = src[c, x, pl.ds(0, size_y, stride=FIELDS), :]
+            new = fade * e0[c, p, :size_y] + rise * (curl[:size_y] - source)
             e[c, p, :size_y] = new
             source = src[c, x, pl.ds(1, size_y, stride=FIELDS), :]
             src1[c, p, :size_y] = source
@@ -595,7 +587,7 @@
                 if comp == c:
                     up_put[n, x] = (new, source)[array][size_y - 2 + r : size_y - 1 + r]
 
-    sweep(0, size_x, own, 4)
+    sweep(0, size_x, own, 8)
     pl.semaphore_wait(barrier, others)
     halos = Exchange(
         place,
@@ -632,13 +624,13 @@
     sweep(0, size_x + 4, unstage, 4)
 
 
-def share(nx, ny, base, state, src, fwd):
-    size_x, size_y, depth = base.shape[1:]
+def share(nx, ny, state, src, fwd):
+    size_x, size_y, depth = fwd.shape[2:]
     wide, tall = size_x + 4, size_y + 8
     return pl.pallas_call(
         functools.partial(share_kernel, nx, ny),
         out_shape=[f32(6, wide, tall, depth), f32(size_x, size_y, depth)],
-        in_specs=in_vmem(4),
+        in_specs=in_vmem(3),
         out_specs=in_vmem(2),
         scratch_shapes=[
             *halo_scratch(SHARE_DOWN, SHARE_UP, size_x, depth),
@@ -649,7 +641,7 @@
             collective_id=1, has_side_effects=True, vmem_limit_bytes=6 * MIB
         ),
         name="share",
-    )(base, state, src, fwd)
+    )(state, src, fwd)
 
 
 def finish_kernel(
@@ -765,7 +757,7 @@
     receivers = receiver_data.shape[0]
     cap = 3 * receivers // (nx * ny)
     by_lane = lambda a: a.reshape(receivers // LANES, LANES)
-    got, codes, state, base = route(
+    got, codes, state = route(
         nx,
         ny,
         receiver_data,
@@ -779,7 +771,7 @@
     )
     placed = scatter(cap, 3 * size_x * size_y, codes, got)
     placed = placed.reshape(3, size_x, size_y * FIELDS, depth)
-    both, grad1 = share(nx, ny, base, state, placed, forward_e)
+    both, grad1 = share(nx, ny, state, placed, forward_e)
     return tuple(finish(nx, ny, both, state, placed, forward_e, grad1))
 
 

time: 39.2 us -> 39 us (level)
  no operation moved by 1% of the time
where the time goes in v7:
time: 39 us; the launch traced here: 38.9 us
  Pallas kernels  38.2 us (98%)
  between operations  0.67 us (2%)
    pallas_call x1, Pallas kernels, route(): pl.pallas_call(functools.partial(route_kernel, nx, ny, size_x * size_y *...  16.5 us
    pallas_call x1, Pallas kernels, share(): pl.pallas_call(functools.partial(share_kernel, nx, ny), out_shape=[f32(6,...  10.3 us
    pallas_call x1, Pallas kernels, scatter(): pl.pallas_call(functools.partial(scatter_kernel, cap), out_shape=jax.Shap...  6.51 us
    pallas_call x1, Pallas kernels, finish(): pl.pallas_call(functools.partial(finish_kernel, nx, ny), out_shape=[field...  4.88 us

profile of v7, /device:TPU:9, one launch (start us, length us, event | category | flops | bytes accessed | tf_op | source)
XLA Modules:
  0.0 38.9 jit_solution(10360658312837469883)
XLA Ops:
  0.6 16.5 %route.1 = (f32[128,128]{1,0:T(8,128)S(1)}, s32[32,128]{1,0:T(8,128)S(1)}, f32[8,36,48,128]{3,2,1,0:T(8,128)S(1)}) custom-call(f32[1024,128]{1,0:T(8,128)} %data_in.1, s32[8,128]{1,0:T(8,128)} %bitcast.6, s32[8,128]{1,0:T(8,128)} %bitcast.7, s32[8,128]{1,0:T(8,128)} %bitcast.8, f32[3,32,40,128]{3,2,1,0:T(8,128)} %e_in.1, f32[3,32,40,128]{3,2,1,0:T(8,128)} %h_in.1, ...), custom_call_target="tpu_custom_call" | custom-call | tf_op jit(solution)/shard_map/route/pallas_call | solution.py:455
  17.2 0.0 copy-start
  17.2 6.5 %scatter.1 = f32[15360,128]{1,0:T(8,128)S(1)} custom-call(s32[32,128]{1,0:T(8,128)S(1)} %get-tuple-element.9.code_in, f32[128,128]{1,0:T(8,128)S(1)} %get-tuple-element.10.got_ref), custom_call_target="tpu_custom_call" | custom-call | tf_op jit(solution)/shard_map/scatter/pallas_call | solution.py:546
  23.7 0.0 copy-done
  23.7 10.3 %share.1 = (f32[6,36,48,128]{3,2,1,0:T(8,128)S(1)}, f32[32,40,128]{2,1,0:T(8,128)S(1)}) custom-call(f32[8,36,48,128]{3,2,1,0:T(8,128)S(1)} %get-tuple-element.8.state, f32[3,32,160,128]{3,2,1,0:T(8,128)S(1)} %bitcast.4, bf16[3,3,32,40,128]{4,3,2,1,0:T(8,128)(2,1)S(1)} %copy-done), custom_call_target="tpu_custom_call" | custom-call | tf_op jit(solution)/shard_map/share/pallas_call | solution.py:630
  34.0 4.9 %finish.1 = (f32[3,32,40,128]{3,2,1,0:T(8,128)}, f32[3,32,40,128]{3,2,1,0:T(8,128)}, f32[32,40,128]{2,1,0:T(8,128)}) custom-call(f32[6,36,48,128]{3,2,1,0:T(8,128)S(1)} %get-tuple-element.11.both, f32[8,36,48,128]{3,2,1,0:T(8,128)S(1)} %get-tuple-element.8.state, f32[3,32,160,128]{3,2,1,0:T(8,128)S(1)} %bitcast.5, bf16[3,3,32,40,128]{4,3,2,1,0:T(8,128)(2,1)S(1)} %copy-done, ...), custom_call_target="tpu_custom_call" | custom-call | tf_op jit(solution)/shard_map/finish/pallas_call | solution.py:728
Async XLA Ops:
  17.2 6.5 %copy-start = (bf16[3,3,32,40,128]{4,3,2,1,0:T(8,128)(2,1)S(1)}, bf16[3,3,32,40,128]{4,3,2,1,0:T(8,128)(2,1)}, u32[]{:S(2)}) copy-start(bf16[3,3,32,40,128]{4,3,2,1,0:T(8,128)(2,1)} %fwd.3) | copy-start | bytes 8847364

commit v8 on v7

--- a/solution.py
+++ b/solution.py
@@ -161,6 +161,14 @@
     curl_z = (e[1, p + 1] - ey) - (up_y(ex) - ex)
     for c, curl in enumerate((curl_x, curl_y, curl_z)):
         h_to[c, p] = h_from[c, p] - factor * curl
+
+
+def h_rows(e, h, p, rows, factor, up_z, up_y):
+    ex, ey, ez = (e[c, p, rows] for c in range(3))
+    curl_x = (up_y(2, ez) - ez) - (up_z(ey) - ey)
+    curl_y = (up_z(ex) - ex) - (e[2, p + 1, rows] - ez)
+    curl_z = (e[1, p + 1, rows] - ey) - (up_y(0, ex) - ex)
+    return [h[c, p, rows] - factor * curl for c, curl in enumerate((curl_x, curl_y, curl_z))]
 
 
 def curl_h(h, p, moves):
@@ -561,7 +569,7 @@
 
 
 def share_kernel(
-    nx, ny, state, src, fwd, both, grad, dn_put, up_put, up_got, lo_got, send, recv
+    nx, ny, state, src, fwd, both, grad, h_low, dn_put, up_put, up_got, lo_got, send, recv
 ):
     place = Place(nx, ny)
     e0, h1, decay, gain = parts_of(state)
@@ -604,6 +612,16 @@
         grad[x] = total
 
     sweep(0, size_x, product, 4)
+
+    low = h_low.shape[2]
+    up_z, _, up_y, _ = shifts(size_y, depth)
+
+    def h_second(x):
+        new = h_rows(e, h1, x + 2, slice(0, size_y), time_step, up_z, lambda c, f: up_y(f))
+        for c in range(3):
+            h_low[c, x] = new[c][:low]
+
+    sweep(0, size_x - 2, h_second, 6)
     halos.wait()
     for p in (0, 1, size_x + 2, size_x + 3):
         keep = place.plane(p, size_x)
@@ -629,9 +647,13 @@
     wide, tall = size_x + 4, size_y + 8
     return pl.pallas_call(
         functools.partial(share_kernel, nx, ny),
-        out_shape=[f32(6, wide, tall, depth), f32(size_x, size_y, depth)],
+        out_shape=[
+            f32(6, wide, tall, depth),
+            f32(size_x, size_y, depth),
+            f32(3, size_x - 2, size_y - 8, depth),
+        ],
         in_specs=in_vmem(3),
-        out_specs=in_vmem(2),
+        out_specs=in_vmem(3),
         scratch_shapes=[
             *halo_scratch(SHARE_DOWN, SHARE_UP, size_x, depth),
             pltpu.SemaphoreType.DMA((8,)),
@@ -645,7 +667,7 @@
 
 
 def finish_kernel(
-    nx, ny, both, state, src, fwd, grad1, e_out, h_out, grad_out, e, h, grad, sem
+    nx, ny, both, state, src, fwd, grad1, h_low, e_out, h_out, grad_out, e, h, grad, sem
 ):
     place = Place(nx, ny)
     e1, src1 = both.at[pl.ds(0, 3)], both.at[pl.ds(3, 3)]
@@ -655,10 +677,24 @@
     moves = shifts(rows, depth)
     factor = h_factor(place, size_y, rows, depth)
 
-    def h_second(p):
+    low = h_low.shape[2]
+    up_z = shifts(rows - low, depth)[0]
+    last = lax.broadcasted_iota(jnp.int32, (rows - low, depth), 0) == rows - low - 1
+
+    def h_second(x):
+        p = x + 2
+
+        def up_y(c, f):
+            return jnp.where(last, e1[c, p, 0:1], pltpu.roll(f, rows - low - 1, 0))
+
+        new = h_rows(e1, h1, p, slice(low, rows), factor[low:], up_z, up_y)
+        for c in range(3):
+            h[c, p, :low] = h_low[c, x]
+            h[c, p, low:] = new[c]
+
+    for p in (0, 1, size_x, size_x + 1, size_x + 2):
         h_plane(e1, h1, h, p, factor * jnp.where(place.plane(p, size_x), 1.0, 0.0), moves)
-
-    sweep(0, size_x + 3, h_second, 7)
+    sweep(0, size_x - 2, h_second, 6)
 
     def e_second(p, inner):
         fade, rise = decay[p], gain[p]
@@ -722,13 +758,13 @@
             copy.wait()
 
 
-def finish(nx, ny, both, state, src, fwd, grad1):
+def finish(nx, ny, both, state, src, fwd, grad1, h_low):
     size_x, size_y, depth = grad1.shape
     field = f32(3, size_x, size_y, depth)
     return pl.pallas_call(
         functools.partial(finish_kernel, nx, ny),
         out_shape=[field, field, f32(size_x, size_y, depth)],
-        in_specs=in_vmem(5),
+        in_specs=in_vmem(6),
         out_specs=[pl.BlockSpec(memory_space=pltpu.HBM)] * 3,
         scratch_shapes=[
             pltpu.VMEM((3, *both.shape[1:]), jnp.float32),
@@ -738,7 +774,7 @@
         ],
         compiler_params=pltpu.CompilerParams(vmem_limit_bytes=10 * MIB),
         name="finish",
-    )(both, state, src, fwd, grad1)
+    )(both, state, src, fwd, grad1, h_low)
 
 
 def per_device(
@@ -771,8 +807,8 @@
     )
     placed = scatter(cap, 3 * size_x * size_y, codes, got)
     placed = placed.reshape(3, size_x, size_y * FIELDS, depth)
-    both, grad1 = share(nx, ny, state, placed, forward_e)
-    return tuple(finish(nx, ny, both, state, placed, forward_e, grad1))
+    both, grad1, h_low = share(nx, ny, state, placed, forward_e)
+    return tuple(finish(nx, ny, both, state, placed, forward_e, grad1, h_low))
 
 
 def solution(mesh):

time: 39 us -> 39.1 us (level)
  no operation moved by 1% of the time
where the time goes in v8:
time: 39.1 us; the launch traced here: 39 us
  Pallas kernels  38.3 us (98%)
  between operations  0.67 us (2%)
    pallas_call x1, Pallas kernels, route(): pl.pallas_call(functools.partial(route_kernel, nx, ny, size_x * size_y *...  16.5 us
    pallas_call x1, Pallas kernels, share(): pl.pallas_call(functools.partial(share_kernel, nx, ny), out_shape=[f32(6,...  10.1 us
    pallas_call x1, Pallas kernels, scatter(): pl.pallas_call(functools.partial(scatter_kernel, cap), out_shape=jax.Shap...  6.86 us
    pallas_call x1, Pallas kernels, finish(): pl.pallas_call(functools.partial(finish_kernel, nx, ny), out_shape=[field...  4.77 us

profile of v8, /device:TPU:9, one launch (start us, length us, event | category | flops | bytes accessed | tf_op | source)
XLA Modules:
  0.0 39.0 jit_solution(17430246530482001466)
XLA Ops:
  0.6 16.5 %route.1 = (f32[128,128]{1,0:T(8,128)S(1)}, s32[32,128]{1,0:T(8,128)S(1)}, f32[8,36,48,128]{3,2,1,0:T(8,128)S(1)}) custom-call(f32[1024,128]{1,0:T(8,128)} %data_in.1, s32[8,128]{1,0:T(8,128)} %bitcast.6, s32[8,128]{1,0:T(8,128)} %bitcast.7, s32[8,128]{1,0:T(8,128)} %bitcast.8, f32[3,32,40,128]{3,2,1,0:T(8,128)} %e_in.1, f32[3,32,40,128]{3,2,1,0:T(8,128)} %h_in.1, ...), custom_call_target="tpu_custom_call" | custom-call | tf_op jit(solution)/shard_map/route/pallas_call | solution.py:463
  17.2 0.0 copy-start
  17.2 6.9 %scatter.1 = f32[15360,128]{1,0:T(8,128)S(1)} custom-call(s32[32,128]{1,0:T(8,128)S(1)} %get-tuple-element.10.code_in, f32[128,128]{1,0:T(8,128)S(1)} %get-tuple-element.11.got_ref), custom_call_target="tpu_custom_call" | custom-call | tf_op jit(solution)/shard_map/scatter/pallas_call | solution.py:554
  24.1 0.0 copy-done
  24.1 10.1 %share.1 = (f32[6,36,48,128]{3,2,1,0:T(8,128)S(1)}, f32[32,40,128]{2,1,0:T(8,128)S(1)}, f32[3,30,32,128]{3,2,1,0:T(8,128)S(1)}) custom-call(f32[8,36,48,128]{3,2,1,0:T(8,128)S(1)} %get-tuple-element.9.state, f32[3,32,160,128]{3,2,1,0:T(8,128)S(1)} %bitcast.4, bf16[3,3,32,40,128]{4,3,2,1,0:T(8,128)(2,1)S(1)} %copy-done), custom_call_target="tpu_custom_call" | custom-call | tf_op jit(solution)/shard_map/share/pallas_call | solution.py:648
  34.2 4.8 %finish.1 = (f32[3,32,40,128]{3,2,1,0:T(8,128)}, f32[3,32,40,128]{3,2,1,0:T(8,128)}, f32[32,40,128]{2,1,0:T(8,128)}) custom-call(f32[6,36,48,128]{3,2,1,0:T(8,128)S(1)} %get-tuple-element.12.both, f32[8,36,48,128]{3,2,1,0:T(8,128)S(1)} %get-tuple-element.9.state, f32[3,32,160,128]{3,2,1,0:T(8,128)S(1)} %bitcast.5, bf16[3,3,32,40,128]{4,3,2,1,0:T(8,128)(2,1)S(1)} %copy-done, ...), custom_call_target="tpu_custom_call" | custom-call | tf_op jit(solution)/shard_map/finish/pallas_call | solution.py:764
Async XLA Ops:
  17.2 6.9 %copy-start = (bf16[3,3,32,40,128]{4,3,2,1,0:T(8,128)(2,1)S(1)}, bf16[3,3,32,40,128]{4,3,2,1,0:T(8,128)(2,1)}, u32[]{:S(2)}) copy-start(bf16[3,3,32,40,128]{4,3,2,1,0:T(8,128)(2,1)} %fwd.3) | copy-start | bytes 8847364

commit v9 on v8

--- a/solution.py
+++ b/solution.py
@@ -14,7 +14,7 @@
 SPAN = LANES // FIELDS
 MESH = pl.DeviceIdType.MESH
 GROUP = 8
-PARTS = 4
+PARTS = 2
 MIB = 1 << 20
 
 time_step = 0.55
@@ -694,7 +694,7 @@
 
     for p in (0, 1, size_x, size_x + 1, size_x + 2):
         h_plane(e1, h1, h, p, factor * jnp.where(place.plane(p, size_x), 1.0, 0.0), moves)
-    sweep(0, size_x - 2, h_second, 6)
+    sweep(0, size_x - 2, h_second, 10)
 
     def e_second(p, inner):
         fade, rise = decay[p], gain[p]
@@ -713,7 +713,7 @@
     def e_inner(p):
         e_second(p, True)
 
-    sweep(2, size_x, e_inner, 8)
+    sweep(2, size_x, e_inner, 16)
     e_second(size_x + 2, False)
 
     def h_third(p):

time: 39.1 us -> 38.5 us (0.985)
  Pallas kernels: 38.3 us -> 37.6 us
    pallas_call x1, Pallas kernels: 10.1 us -> 9.67 us  [share(): pl.pallas_call(functools.partial(share_kernel, nx, ny), out_shape=[f32(6,...]
where the time goes in v9:
time: 38.5 us; the launch traced here: 38.2 us
  Pallas kernels  37.6 us (98%)
  between operations  0.67 us (2%)
    pallas_call x1, Pallas kernels, route(): pl.pallas_call(functools.partial(route_kernel, nx, ny, size_x * size_y *...  16.5 us
    pallas_call x1, Pallas kernels, share(): pl.pallas_call(functools.partial(share_kernel, nx, ny), out_shape=[f32(6,...  9.67 us
    pallas_call x1, Pallas kernels, scatter(): pl.pallas_call(functools.partial(scatter_kernel, cap), out_shape=jax.Shap...  6.87 us
    pallas_call x1, Pallas kernels, finish(): pl.pallas_call(functools.partial(finish_kernel, nx, ny), out_shape=[field...  4.5 us

profile of v9, /device:TPU:9, one launch (start us, length us, event | category | flops | bytes accessed | tf_op | source)
XLA Modules:
  0.0 38.2 jit_solution(9989532166006808419)
XLA Ops:
  0.6 16.5 %route.1 = (f32[128,128]{1,0:T(8,128)S(1)}, s32[32,128]{1,0:T(8,128)S(1)}, f32[8,36,48,128]{3,2,1,0:T(8,128)S(1)}) custom-call(f32[1024,128]{1,0:T(8,128)} %data_in.1, s32[8,128]{1,0:T(8,128)} %bitcast.6, s32[8,128]{1,0:T(8,128)} %bitcast.7, s32[8,128]{1,0:T(8,128)} %bitcast.8, f32[3,32,40,128]{3,2,1,0:T(8,128)} %e_in.1, f32[3,32,40,128]{3,2,1,0:T(8,128)} %h_in.1, ...), custom_call_target="tpu_custom_call" | custom-call | tf_op jit(solution)/shard_map/route/pallas_call | solution.py:463
  17.2 0.0 copy-start
  17.2 6.9 %scatter.1 = f32[15360,128]{1,0:T(8,128)S(1)} custom-call(s32[32,128]{1,0:T(8,128)S(1)} %get-tuple-element.10.code_in, f32[128,128]{1,0:T(8,128)S(1)} %get-tuple-element.11.got_ref), custom_call_target="tpu_custom_call" | custom-call | tf_op jit(solution)/shard_map/scatter/pallas_call | solution.py:554
  24.1 0.0 copy-done
  24.1 9.7 %share.1 = (f32[6,36,48,128]{3,2,1,0:T(8,128)S(1)}, f32[32,40,128]{2,1,0:T(8,128)S(1)}, f32[3,30,32,128]{3,2,1,0:T(8,128)S(1)}) custom-call(f32[8,36,48,128]{3,2,1,0:T(8,128)S(1)} %get-tuple-element.9.state, f32[3,32,160,128]{3,2,1,0:T(8,128)S(1)} %bitcast.4, bf16[3,3,32,40,128]{4,3,2,1,0:T(8,128)(2,1)S(1)} %copy-done), custom_call_target="tpu_custom_call" | custom-call | tf_op jit(solution)/shard_map/share/pallas_call | solution.py:648
  33.7 4.5 %finish.1 = (f32[3,32,40,128]{3,2,1,0:T(8,128)}, f32[3,32,40,128]{3,2,1,0:T(8,128)}, f32[32,40,128]{2,1,0:T(8,128)}) custom-call(f32[6,36,48,128]{3,2,1,0:T(8,128)S(1)} %get-tuple-element.12.both, f32[8,36,48,128]{3,2,1,0:T(8,128)S(1)} %get-tuple-element.9.state, f32[3,32,160,128]{3,2,1,0:T(8,128)S(1)} %bitcast.5, bf16[3,3,32,40,128]{4,3,2,1,0:T(8,128)(2,1)S(1)} %copy-done, ...), custom_call_target="tpu_custom_call" | custom-call | tf_op jit(solution)/shard_map/finish/pallas_call | solution.py:764
Async XLA Ops:
  17.2 6.9 %copy-start = (bf16[3,3,32,40,128]{4,3,2,1,0:T(8,128)(2,1)S(1)}, bf16[3,3,32,40,128]{4,3,2,1,0:T(8,128)(2,1)}, u32[]{:S(2)}) copy-start(bf16[3,3,32,40,128]{4,3,2,1,0:T(8,128)(2,1)} %fwd.3) | copy-start | bytes 8847364

commit v10 on v9

--- a/solution.py
+++ b/solution.py
@@ -401,7 +401,7 @@
                     array, c, p, ROUTE_DOWN, ROUTE_UP, up_got, lo_got, above, below, gap
                 )
 
-    sweep(0, size_x + 4, unstage, 4)
+    sweep(0, size_x + 4, unstage, 12)
     row = lax.broadcasted_iota(jnp.int32, (rows, depth), 0)
     inside = jnp.where(
         row < size_y,
@@ -424,7 +424,7 @@
         decay[p] = jnp.where(keep, (eps - half_loss) * inverse, 0.0)
         gain[p] = jnp.where(keep, time_step * inverse, 0.0)
 
-    sweep(1, size_x + 2, coefficients, 2)
+    sweep(1, size_x + 2, coefficients, 17)
     moves = shifts(rows, depth)
     factor = h_factor(place, size_y, rows, depth)
 
@@ -639,7 +639,7 @@
                     array, c, p, SHARE_DOWN, SHARE_UP, up_got, lo_got, above, below, gap
                 )
 
-    sweep(0, size_x + 4, unstage, 4)
+    sweep(0, size_x + 4, unstage, 12)
 
 
 def share(nx, ny, state, src, fwd):

time: 38.5 us -> 38.5 us (level)
  no operation moved by 1% of the time
where the time goes in v10:
time: 38.5 us; the launch traced here: 38.2 us
  Pallas kernels  37.5 us (97%)
  between operations  0.67 us (2%)
    pallas_call x1, Pallas kernels, route(): pl.pallas_call(functools.partial(route_kernel, nx, ny, size_x * size_y *...  16.5 us
    pallas_call x1, Pallas kernels, share(): pl.pallas_call(functools.partial(share_kernel, nx, ny), out_shape=[f32(6,...  9.63 us
    pallas_call x1, Pallas kernels, scatter(): pl.pallas_call(functools.partial(scatter_kernel, cap), out_shape=jax.Shap...  6.87 us
    pallas_call x1, Pallas kernels, finish(): pl.pallas_call(functools.partial(finish_kernel, nx, ny), out_shape=[field...  4.5 us

profile of v10, /device:TPU:9, one launch (start us, length us, event | category | flops | bytes accessed | tf_op | source)
XLA Modules:
  0.0 38.2 jit_solution(4309566906339868143)
XLA Ops:
  0.6 16.5 %route.1 = (f32[128,128]{1,0:T(8,128)S(1)}, s32[32,128]{1,0:T(8,128)S(1)}, f32[8,36,48,128]{3,2,1,0:T(8,128)S(1)}) custom-call(f32[1024,128]{1,0:T(8,128)} %data_in.1, s32[8,128]{1,0:T(8,128)} %bitcast.6, s32[8,128]{1,0:T(8,128)} %bitcast.7, s32[8,128]{1,0:T(8,128)} %bitcast.8, f32[3,32,40,128]{3,2,1,0:T(8,128)} %e_in.1, f32[3,32,40,128]{3,2,1,0:T(8,128)} %h_in.1, ...), custom_call_target="tpu_custom_call" | custom-call | tf_op jit(solution)/shard_map/route/pallas_call | solution.py:463
  17.2 0.0 copy-start
  17.2 6.9 %scatter.1 = f32[15360,128]{1,0:T(8,128)S(1)} custom-call(s32[32,128]{1,0:T(8,128)S(1)} %get-tuple-element.10.code_in, f32[128,128]{1,0:T(8,128)S(1)} %get-tuple-element.11.got_ref), custom_call_target="tpu_custom_call" | custom-call | tf_op jit(solution)/shard_map/scatter/pallas_call | solution.py:554
  24.1 0.0 copy-done
  24.1 9.6 %share.1 = (f32[6,36,48,128]{3,2,1,0:T(8,128)S(1)}, f32[32,40,128]{2,1,0:T(8,128)S(1)}, f32[3,30,32,128]{3,2,1,0:T(8,128)S(1)}) custom-call(f32[8,36,48,128]{3,2,1,0:T(8,128)S(1)} %get-tuple-element.9.state, f32[3,32,160,128]{3,2,1,0:T(8,128)S(1)} %bitcast.4, bf16[3,3,32,40,128]{4,3,2,1,0:T(8,128)(2,1)S(1)} %copy-done), custom_call_target="tpu_custom_call" | custom-call | tf_op jit(solution)/shard_map/share/pallas_call | solution.py:648
  33.7 4.5 %finish.1 = (f32[3,32,40,128]{3,2,1,0:T(8,128)}, f32[3,32,40,128]{3,2,1,0:T(8,128)}, f32[32,40,128]{2,1,0:T(8,128)}) custom-call(f32[6,36,48,128]{3,2,1,0:T(8,128)S(1)} %get-tuple-element.12.both, f32[8,36,48,128]{3,2,1,0:T(8,128)S(1)} %get-tuple-element.9.state, f32[3,32,160,128]{3,2,1,0:T(8,128)S(1)} %bitcast.5, bf16[3,3,32,40,128]{4,3,2,1,0:T(8,128)(2,1)S(1)} %copy-done, ...), custom_call_target="tpu_custom_call" | custom-call | tf_op jit(solution)/shard_map/finish/pallas_call | solution.py:764
Async XLA Ops:
  17.2 6.9 %copy-start = (bf16[3,3,32,40,128]{4,3,2,1,0:T(8,128)(2,1)S(1)}, bf16[3,3,32,40,128]{4,3,2,1,0:T(8,128)(2,1)}, u32[]{:S(2)}) copy-start(bf16[3,3,32,40,128]{4,3,2,1,0:T(8,128)(2,1)} %fwd.3) | copy-start | bytes 8847364
